TPU v7x, 32 devices: a whole 2x2x4 slice. The times are simulated.
32 devices in a mesh: docs: 16 (over z, y, x), heads: 2 (over core).
Axes of the slice: x: 2, y: 2, z: 4, core: 2. Of those that a mesh axis runs over, the one named last changes fastest.
Arguments:
- tokens: bfloat16 [32768, 768], P('docs'), may hold values from -6 to 6
- grad_out: float32 [32768, 768], P('docs'), may hold values from -6 to 6
- live_tokens: int32 [16], P('docs'), may hold values from 1024 to 2048, as said below
- w_qkv: bfloat16 [768, 3, 768], P(None, None, 'heads'), may hold values from -0.21875 to 0.21875
- b_qv: float32 [2, 768], P(None, 'heads'), may hold values from -3 to 3
- w_out: bfloat16 [768, 768], P('heads'), may hold values from -0.875 to 0.875
- b_out: float32 [768], replicated, may hold values from -3 to 3
- gain_one: float32 [768], replicated, may hold values from 0.25 to 1.75
- shift_one: float32 [768], replicated, may hold values from -3 to 3
- w_up: bfloat16 [768, 3072], P(None, 'heads'), may hold values from -0.21875 to 0.21875
- b_up: float32 [3072], P('heads'), may hold values from -3 to 3
- w_down: bfloat16 [3072, 768], P('heads'), may hold values from -0.15625 to 0.15625
- b_down: float32 [768], replicated, may hold values from -3 to 3
- gain_two: float32 [768], replicated, may hold values from 0.25 to 1.75
- shift_two: float32 [768], replicated, may hold values from -3 to 3
Outputs:
- layer_out: float32 [32768, 768], P('docs')
- d_tokens: float32 [32768, 768], P('docs')
- d_w_qkv: float32 [768, 3, 768], P('docs', None, 'heads')
- d_b_qv: float32 [2, 768], P(None, 'heads')
- d_w_out: float32 [768, 768], P('heads', 'docs')
- d_b_out: float32 [768], replicated
- d_gain_one: float32 [768], replicated
- d_shift_one: float32 [768], replicated
- d_w_up: float32 [768, 3072], P('docs', 'heads')
- d_b_up: float32 [3072], P('heads')
- d_w_down: float32 [3072, 768], P('heads', 'docs')
- d_b_down: float32 [768], replicated
- d_gain_two: float32 [768], replicated
- d_shift_two: float32 [768], replicated
Inputs may be any that keep to these rules, and one draw needn't show every extreme that they name: `live_tokens`: live tokens of each group; slots from there on are padding. Some group holds exactly 2048 and some exactly 1024.
All inputs are finite; a program needn't handle non-finite values.
Results may differ from a plain program's by a relative error of at most 0.02.
The roundings to bfloat16 on the way count: a program that leaves them out, or rounds other values in their place, can miss the bound.
Values may be sent and summed in bfloat16 or wider, within the bound.
No kernel may reach another device: no remote copies, remote signals or barrier semaphores. Data moves between devices by JAX's collectives and lax.ppermute only.
A program may use at most 192 MiB of HBM per device.

v0:
```python
import jax
import jax.numpy as jnp
from jax import lax
from jax.sharding import PartitionSpec as P

HEAD_DIM = 64
SEG = 128


def layer_norm(values, gain, shift):
    center = values - jnp.mean(values, -1, keepdims=True)
    spread = jnp.mean(center * center, -1, keepdims=True)
    return center * lax.rsqrt(spread + 1e-05) * gain + shift


def gelu_exact(values):
    return 0.5 * values * (1.0 + jax.scipy.special.erf(values * 0.7071067811865476))


def left_dot(first, second):
    return lax.dot_general(
        first, second, (((0,), (0,)), ((), ())), preferred_element_type=jnp.float32
    )


def right_dot(first, second):
    return lax.dot_general(
        first, second, (((1,), (1,)), ((), ())), preferred_element_type=jnp.float32
    )


def shards(
    tokens,
    grad_out,
    live_tokens,
    w_qkv,
    b_qv,
    w_out,
    b_out,
    gain_one,
    shift_one,
    w_up,
    b_up,
    w_down,
    b_down,
    gain_two,
    shift_two,
):
    count_rows, width = tokens.shape
    local_cols = w_qkv.shape[2]
    local_heads = local_cols // HEAD_DIM
    segments = count_rows // SEG
    scale = HEAD_DIM ** (-0.5)
    row_mask = lax.iota(jnp.int32, count_rows) < live_tokens[0]
    key_bias = jnp.where(row_mask, 0.0, -30000.0).astype(jnp.float32).reshape(segments, 1, 1, SEG)
    shape_four = (segments, SEG, local_heads, HEAD_DIM)
    flat_qkv = w_qkv.reshape(width, 3 * local_cols)
    linear = jnp.dot(tokens, flat_qkv, preferred_element_type=jnp.float32).reshape(
        count_rows, 3, local_cols
    )
    query_blocks = (linear[:, 0] + b_qv[0]).astype(jnp.bfloat16).reshape(shape_four)
    key_blocks = linear[:, 1].astype(jnp.bfloat16).reshape(shape_four)
    value_blocks = (linear[:, 2] + b_qv[1]).astype(jnp.bfloat16).reshape(shape_four)

    def scores_of():
        raw = jnp.einsum(
            "sqhd,skhd->shqk", query_blocks, key_blocks, preferred_element_type=jnp.float32
        )
        return raw * scale + key_bias

    scores = scores_of()
    top_score = jnp.max(scores, -1, keepdims=True)
    exp_scores = jnp.exp(scores - top_score)
    totals = jnp.sum(exp_scores, -1, keepdims=True)
    probs_low = (exp_scores / totals).astype(jnp.bfloat16)
    log_total = top_score + jnp.log(totals)
    attended = jnp.einsum(
        "shqk,skhd->sqhd", probs_low, value_blocks, preferred_element_type=jnp.float32
    )
    attended = attended.reshape(count_rows, local_cols).astype(jnp.bfloat16)
    attn_part = jnp.dot(attended, w_out, preferred_element_type=jnp.float32)
    attn_sum = lax.psum(attn_part.astype(jnp.bfloat16), "heads").astype(jnp.float32)
    first_sum = tokens.astype(jnp.float32) + attn_sum + b_out
    normed_one, first_back = jax.vjp(layer_norm, first_sum, gain_one, shift_one)
    normed_low = normed_one.astype(jnp.bfloat16)
    pre = jnp.dot(normed_low, w_up, preferred_element_type=jnp.float32) + b_up
    hidden_full, gelu_back = jax.vjp(gelu_exact, pre)
    hidden = hidden_full.astype(jnp.bfloat16)
    mlp_part = jnp.dot(hidden, w_down, preferred_element_type=jnp.float32)
    mlp_sum = lax.psum(mlp_part.astype(jnp.bfloat16), "heads").astype(jnp.float32)
    second_sum = normed_one + mlp_sum + b_down
    layer_out, second_back = jax.vjp(layer_norm, second_sum, gain_two, shift_two)
    cotangent = jnp.where(row_mask[:, None], grad_out, 0.0)
    d_second, d_gain_two, d_shift_two = second_back(cotangent)
    d_b_down = jnp.sum(d_second, 0)
    d_mlp = d_second.astype(jnp.bfloat16)
    d_w_down = left_dot(hidden, d_mlp)
    d_hidden = right_dot(d_mlp, w_down)
    (d_pre_full,) = gelu_back(d_hidden)
    d_pre = d_pre_full.astype(jnp.bfloat16)
    d_b_up = jnp.sum(d_pre.astype(jnp.float32), 0)
    d_w_up = left_dot(normed_low, d_pre)
    d_normed = d_second + lax.psum(right_dot(d_pre, w_up).astype(jnp.bfloat16), "heads").astype(
        jnp.float32
    )
    d_first, d_gain_one, d_shift_one = first_back(d_normed)
    d_b_out = jnp.sum(d_first, 0)
    d_branch = d_first.astype(jnp.bfloat16)
    d_w_out = left_dot(attended, d_branch)
    d_attended = right_dot(d_branch, w_out).astype(jnp.bfloat16).reshape(shape_four)
    probs = jnp.exp(scores_of() - log_total)
    d_probs = jnp.einsum(
        "sqhd,skhd->shqk", d_attended, value_blocks, preferred_element_type=jnp.float32
    )
    d_scores = (probs * (d_probs - jnp.sum(probs * d_probs, -1, keepdims=True))).astype(
        jnp.bfloat16
    )
    d_values = jnp.einsum(
        "shqk,sqhd->skhd",
        probs.astype(jnp.bfloat16),
        d_attended,
        preferred_element_type=jnp.float32,
    )
    d_query = (
        jnp.einsum("shqk,skhd->sqhd", d_scores, key_blocks, preferred_element_type=jnp.float32)
        * scale
    )
    d_keys = (
        jnp.einsum("shqk,sqhd->skhd", d_scores, query_blocks, preferred_element_type=jnp.float32)
        * scale
    )
    d_linear = jnp.stack(
        [
            d_query.reshape(count_rows, local_cols),
            d_keys.reshape(count_rows, local_cols),
            d_values.reshape(count_rows, local_cols),
        ],
        1,
    ).astype(jnp.bfloat16)
    d_b_qv = jnp.stack(
        [
            jnp.sum(d_linear[:, 0].astype(jnp.float32), 0),
            jnp.sum(d_linear[:, 2].astype(jnp.float32), 0),
        ]
    )
    flat_grad = d_linear.reshape(count_rows, 3 * local_cols)
    d_w_qkv = left_dot(tokens, flat_grad).reshape(width, 3, local_cols)
    d_tokens = d_first + lax.psum(
        right_dot(flat_grad, flat_qkv).astype(jnp.bfloat16), "heads"
    ).astype(jnp.float32)
    d_w_qkv, d_w_out, d_w_up, d_w_down = (
        lax.psum_scatter(d_w_qkv, "docs", scatter_dimension=0, tiled=True),
        lax.psum_scatter(d_w_out, "docs", scatter_dimension=1, tiled=True),
        lax.psum_scatter(d_w_up, "docs", scatter_dimension=0, tiled=True),
        lax.psum_scatter(d_w_down, "docs", scatter_dimension=1, tiled=True),
    )
    d_b_qv, d_b_out, d_gain_one, d_shift_one, d_b_up, d_b_down, d_gain_two, d_shift_two = lax.psum(
        (d_b_qv, d_b_out, d_gain_one, d_shift_one, d_b_up, d_b_down, d_gain_two, d_shift_two),
        "docs",
    )
    return (
        layer_out,
        d_tokens,
        d_w_qkv,
        d_b_qv,
        d_w_out,
        d_b_out,
        d_gain_one,
        d_shift_one,
        d_w_up,
        d_b_up,
        d_w_down,
        d_b_down,
        d_gain_two,
        d_shift_two,
    )


def solution(mesh):
    placed = (
        P("docs", None),
        P("docs", None),
        P("docs"),
        P(None, None, "heads"),
        P(None, "heads"),
        P("heads", None),
        P(),
        P(),
        P(),
        P(None, "heads"),
        P("heads"),
        P("heads", None),
        P(),
        P(),
        P(),
    )
    return jax.shard_map(
        shards,
        mesh=mesh,
        in_specs=placed,
        out_specs=(
            P("docs", None),
            P("docs", None),
            P("docs", None, "heads"),
            P(None, "heads"),
            P("heads", "docs"),
            P(),
            P(),
            P(),
            P("docs", "heads"),
            P("heads"),
            P("heads", "docs"),
            P(),
            P(),
            P(),
        ),
        check_vma=False,
    )
```

profile of v0, /device:TPU:0, one launch (start us, length us, event | category | flops | bytes accessed | tf_op | source)
XLA Modules:
  0.0 858.3 jit_solution(14391557114792816477)
XLA Ops:
  11.2 6.8 fusion.7
  56.4 26.0 %all-reduce.6.cloned.1.call-done = bf16[2048,768]{1,0:T(8,128)(2,1)} async-done(((bf16[2048,768]{1,0:T(8,128)(2,1)}), bf16[2048,768]{1,0:T(8,128)(2,1)}) %all-reduce.6.cloned.1.call-update) | async-done | bytes 3145744 | tf_op jit(solution)/shard_map/psum | solution.py:82
  88.9 9.6 %multiply_convert_fusion = (bf16[2048,1536]{1,0:T(8,128)(2,1)S(1)}, f32[2048,1536]{1,0:T(8,128)}) fusion(f32[1536]{0:T(1024)S(1)} %copy-done.31, bf16[768,1536]{1,0:T(8,128)(2,1)S(1)} %copy-done, f32[768]{0:T(1024)S(1)} %copy-done.26, f32[768]{0:T(1024)S(1)} %copy-done.22, f32[2048]{0:T(1024)S(1)} %fusion.32, f32[2048]{0:T(1024)S(1)} %broadcast_multiply_fusion.1, ...), kind=kOutput, calls=%fused_computation.2 | convolution fusion | flops 4864868352 | bytes 27556864 | tf_op jit(solution)/shard_map/dot_general | solution.py:86
  101.1 6.3 convolution_convert_fusion.2
  107.6 24.5 %all-reduce.8.cloned.1.call-done = bf16[2048,768]{1,0:T(8,128)(2,1)} async-done(((bf16[2048,768]{1,0:T(8,128)(2,1)}), bf16[2048,768]{1,0:T(8,128)(2,1)}) %all-reduce.8.cloned.1.call-update) | async-done | bytes 3145744 | tf_op jit(solution)/shard_map/psum | solution.py:90
  132.0 5.8 fusion.44
  148.7 13.7 %convert_reduce_fusion = (f32[1536]{0:T(1024)S(1)}, bf16[2048,1536]{1,0:T(8,128)(2,1)S(1)}) fusion(bf16[1536,768]{1,0:T(8,128)(2,1)S(1)} %copy-done.29, f32[2048,768]{1,0:T(8,128)S(1)} %get-tuple-element.36, f32[2048]{0:T(1024)S(1)} %negate_multiply_fusion.1, f32[2048,1536]{1,0:T(8,128)} %get-tuple-element.47, f32[1536]{0:T(1024)S(1)} %copy-done.31), kind=kOutput, calls=%fused_computation | convolution fusion | flops 4885314048 | bytes 27545600 | tf_op jit(solution)/shard_map/dot_general | solution.py:27
  165.1 6.4 convolution_convert_fusion.1
  171.6 24.5 %all-reduce.10.cloned.1.call-done = bf16[2048,768]{1,0:T(8,128)(2,1)} async-done(((bf16[2048,768]{1,0:T(8,128)(2,1)}), bf16[2048,768]{1,0:T(8,128)(2,1)}) %all-reduce.10.cloned.1.call-update) | async-done | bytes 3145744 | tf_op jit(solution)/shard_map/psum | solution.py:103
  196.1 7.7 multiply_reduce_fusion.1
  204.4 6.0 fusion.42
  268.9 5.7 bitcast_convert_fusion
  274.6 5.8 fusion.16
  280.6 11.9 %fusion.34 = f32[1536,768]{0,1:T(8,128)} fusion(bf16[2048,1536]{1,0:T(8,128)(2,1)} %copy-done.32, f32[2048,768]{1,0:T(8,128)} %copy-done.7, f32[2048]{0:T(1024)S(1)} %negate_multiply_fusion.1), kind=kOutput, calls=%fused_computation.87 | convolution fusion | flops 4834983936 | bytes 17309696 | tf_op jit(solution)/shard_map/dot_general | solution.py:21
  292.7 14.0 %fusion.35 = f32[768,1536]{1,0:T(8,128)} fusion(bf16[2048,1536]{1,0:T(8,128)(2,1)} %copy-done.33, f32[768]{0:T(1024)S(1)} %copy-done.26, f32[768]{0:T(1024)S(1)} %copy-done.22, f32[2048]{0:T(1024)S(1)} %fusion.32, bf16[2048,768]{1,0:T(8,128)(2,1)} %all-reduce.6.cloned.1.call-done, bf16[2048,768]{1,0:T(8,128)(2,1)} %param.15, ...), kind=kOutput, calls=%fused_computation.88 | convolution fusion | flops 4845993984 | bytes 17327104 | tf_op jit(solution)/shard_map/dot_general | solution.py:21
  306.8 6.6 copy.64
  313.4 9.0 %fusion.47 = f32[1152,768]{1,0:T(8,128)} fusion(bf16[2048,1152]{0,1:T(8,128)(2,1)} %bitcast.101, bf16[2048,768]{1,0:T(8,128)(2,1)} %param.15), kind=kOutput, calls=%fused_computation.96 | convolution fusion | flops 3623878656 | bytes 11403264 | tf_op jit(solution)/shard_map/dot_general | solution.py:21
  322.4 5.2 copy.65
  330.2 6.1 add_reduce_fusion
  336.2 77.7 %all-reduce = (f32[2,384]{1,0:T(2,128)}, f32[768]{0:T(1024)}, f32[768]{0:T(1024)}, f32[768]{0:T(1024)}, f32[1536]{0:T(1024)}, /*index=5*/f32[768]{0:T(1024)}, f32[768]{0:T(1024)}, f32[768]{0:T(1024)}) all-reduce(f32[2,384]{1,0:T(2,128)S(1)} %pad_maximum_fusion, ...), channel_id=1, replica_groups=mesh['docs'=16,'heads'=2] {'docs'}, use_global_device_ids=true, to_apply=%region_18.19 | all-reduce | flops 6912 | bytes 55296 | tf_op jit(solution)/shard_map/psum | solution.py:157
  413.9 15.2 %reduce-scatter.7.cloned.1.call-done = f32[384,48]{0,1:T(8,128)} async-done(((f32[384,768]{0,1:T(8,128)}), f32[384,48]{0,1:T(8,128)}) %reduce-scatter.7.cloned.1.call-update) | async-done | bytes 73744 | tf_op jit(solution)/shard_map/reduce_scatter | solution.py:153
  429.2 141.5 %reduce-scatter.11.cloned.1.call-done = f32[1536,48]{0,1:T(8,128)} async-done(((f32[1536,768]{0,1:T(8,128)}), f32[1536,48]{0,1:T(8,128)}) %reduce-scatter.11.cloned.1.call-update) | async-done | bytes 294928 | tf_op jit(solution)/shard_map/reduce_scatter | solution.py:155
  570.6 142.4 %reduce-scatter.9.cloned.1.call-done = f32[48,1536]{1,0:T(8,128)} async-done(((f32[768,1536]{1,0:T(8,128)}), f32[48,1536]{1,0:T(8,128)}) %reduce-scatter.9.cloned.1.call-update) | async-done | bytes 294928 | tf_op jit(solution)/shard_map/reduce_scatter | solution.py:154
  713.0 137.9 %reduce-scatter.5.cloned.1.call-done = f32[48,3,384]{2,0,1:T(8,128)} async-done(((f32[768,3,384]{2,0,1:T(8,128)}), f32[48,3,384]{2,0,1:T(8,128)}) %reduce-scatter.5.cloned.1.call-update) | async-done | bytes 221200 | tf_op jit(solution)/shard_map/reduce_scatter | solution.py:152
  (152 shorter events, 126.0 us)
Async XLA Ops:
  7.2 81.7 %copy-start = (bf16[768,1536]{1,0:T(8,128)(2,1)S(1)}, bf16[768,1536]{1,0:T(8,128)(2,1)}, u32[]{:S(2)}) copy-start(bf16[768,1536]{1,0:T(8,128)(2,1)} %param.24) | copy-start | bytes 7077892
  7.2 75.2 %all-reduce.6.cloned.1.call-start = ((), (), s32[]{:S(2)}) async-start(), calls=%async_computation.4 | async-start | bytes 6291456 | tf_op jit(solution)/shard_map/psum | solution.py:82
  52.8 29.6 %copy-start.21 = (f32[768]{0:T(1024)S(1)}, f32[768]{0:T(1024)}, u32[]{:S(2)}) copy-start(f32[768]{0:T(1024)} %param.21) | copy-start | bytes 9220
  56.3 32.5 %copy-start.22 = (f32[768]{0:T(1024)S(1)}, f32[768]{0:T(1024)}, u32[]{:S(2)}) copy-start(f32[768]{0:T(1024)} %param.22) | copy-start | bytes 9220
  56.3 32.5 %copy-start.26 = (f32[768]{0:T(1024)S(1)}, f32[768]{0:T(1024)}, u32[]{:S(2)}) copy-start(f32[768]{0:T(1024)} %param.23) | copy-start | bytes 9220
  56.4 32.5 %copy-start.31 = (f32[1536]{0:T(1024)S(1)}, f32[1536]{0:T(1024)}, u32[]{:S(2)}) copy-start(f32[1536]{0:T(1024)} %param.25) | copy-start | bytes 18436
  56.4 75.7 %all-reduce.8.cloned.1.call-start = ((), (), s32[]{:S(2)}) async-start(), calls=%async_computation.5 | async-start | bytes 6291456 | tf_op jit(solution)/shard_map/psum | solution.py:90
  88.9 12.2 %copy-start.28 = (bf16[1536,768]{1,0:T(8,128)(2,1)S(1)}, bf16[1536,768]{1,0:T(8,128)(2,1)}, u32[]{:S(2)}) copy-start(bf16[1536,768]{1,0:T(8,128)(2,1)} %param.26) | copy-start | bytes 7077892
  101.1 30.9 %copy-start.24 = (f32[768]{0:T(1024)S(1)}, f32[768]{0:T(1024)}, u32[]{:S(2)}) copy-start(f32[768]{0:T(1024)} %param.27) | copy-start | bytes 9220
  107.5 88.6 %all-reduce.10.cloned.1.call-start = ((), (), s32[]{:S(2)}) async-start(), calls=%async_computation.6 | async-start | bytes 6291456 | tf_op jit(solution)/shard_map/psum | solution.py:103
  137.8 5.9 slice-start.2
  148.7 13.7 %copy-start.7 = (f32[2048,768]{1,0:T(8,128)}, f32[2048,768]{1,0:T(8,128)S(1)}, u32[]{:S(2)}) copy-start(f32[2048,768]{1,0:T(8,128)S(1)} %get-tuple-element.36) | copy-start | bytes 18874372
  171.5 158.6 %all-reduce.12.cloned.1.call-start = ((), (), s32[]{:S(2)}) async-start(), calls=%async_computation.7 | async-start | bytes 6291456 | tf_op jit(solution)/shard_map/psum | solution.py:148
  196.1 7.8 copy-start.4
  196.1 7.8 copy-start.6
  196.1 8.3 copy-start.14
  216.8 7.2 slice-start
  216.8 7.2 copy-start.17
  268.9 5.8 copy-start.20
  274.6 154.6 %reduce-scatter.7.cloned.1.call-start = ((), (), s32[]{:S(2)}) async-start(), calls=%async_computation.9 | async-start | bytes 1253376 | tf_op jit(solution)/shard_map/reduce_scatter | solution.py:153
  280.5 290.1 %reduce-scatter.11.cloned.1.call-start = ((), (), s32[]{:S(2)}) async-start(), calls=%async_computation.11 | async-start | bytes 5013504 | tf_op jit(solution)/shard_map/reduce_scatter | solution.py:155
  292.4 420.6 %reduce-scatter.9.cloned.1.call-start = ((), (), s32[]{:S(2)}) async-start(), calls=%async_computation.10 | async-start | bytes 5013504 | tf_op jit(solution)/shard_map/reduce_scatter | solution.py:154
  306.7 544.3 %reduce-scatter.5.cloned.1.call-start = ((), (), s32[]{:S(2)}) async-start(), calls=%async_computation.8 | async-start | bytes 3760128 | tf_op jit(solution)/shard_map/reduce_scatter | solution.py:152
  330.1 520.9 %copy-start.1 = (bf16[768,1536]{1,0:T(8,128)(2,1)S(1)}, bf16[768,1536]{1,0:T(8,128)(2,1)}, u32[]{:S(2)}) copy-start(bf16[768,1536]{1,0:T(8,128)(2,1)} %param.24) | copy-start | bytes 7077892
  (22 other events, 79.4 us)
Sparse Core Ops, SparseCore 0:
  56.5 25.8 all-reduce.5
  107.6 24.3 all-reduce.7
  171.7 24.3 all-reduce.9
  274.7 24.3 all-reduce.11
  304.3 124.8 reduce-scatter.6
  434.8 135.8 reduce-scatter.10
  577.2 135.8 reduce-scatter.8
  718.7 132.2 reduce-scatter.4
where the time goes:
time: 866 us; the launch traced here: 858 us
  waiting for transfers between devices  512 us (59%)
  matrix products  115 us (13%)
  local copies, waits for them, and re-layouts  82.7 us (10%)
  blocking collectives  77.7 us (9%)
  other arithmetic  54.4 us (6%)
  between operations  15.9 us (2%)
    reduce_scatter x1, waiting for transfers between devices, shards(): lax.psum_scatter(d_w_up, 'docs', scatter_dimension=0, tiled=True)  142 us
    reduce_scatter x1, waiting for transfers between devices, shards(): lax.psum_scatter(d_w_down, 'docs', scatter_dimension=1, tiled=True)  141 us
    reduce_scatter x1, waiting for transfers between devices, shards(): lax.psum_scatter(d_w_qkv, 'docs', scatter_dimension=0, tiled=True)  138 us
    psum x1, blocking collectives, shards(): lax.psum((d_b_qv, d_b_out, d_gain_one, d_shift_one, d_b_up, d_b_down, d_g...  77.7 us
    dot_general x4, matrix products, left_dot(): lax.dot_general(first, second, (((0,), (0,)), ((), ())), preferred_elemen...  40.7 us
    unnamed x81, local copies, waits for them, and re-layouts  28.8 us
    dot_general x4, matrix products, right_dot(): lax.dot_general(first, second, (((1,), (1,)), ((), ())), preferred_elemen...  27.7 us
    psum x1, waiting for transfers between devices, shards(): lax.psum(attn_part.astype(jnp.bfloat16), 'heads').astype(jnp.float32)  26 us
  transfers between devices with their start and end apart: 8, of which 7 were waited for; matrix products, arithmetic and copies ran while one was open for 7% of the time, Pallas kernels for 0%

commit v1 on v0

v1 whole, which is shorter than its diff:
```python
import functools

import jax
import jax.numpy as jnp
from jax import lax
from jax.experimental import pallas as pl
from jax.experimental.pallas import tpu as pltpu
from jax.sharding import PartitionSpec as P

HEAD_DIM = 64
SEG = 128
EPS = 1e-05
LANES = 128
F32 = jnp.float32
LOW = jnp.bfloat16
OWN = jnp.float32
BWD_CHUNK = 768
VMEM_LIMIT = 60 * 1024 * 1024


def mm(first, second):
    return jnp.dot(first, second, preferred_element_type=F32)


def mm_nt(first, second):
    return lax.dot_general(first, second, (((1,), (1,)), ((), ())), preferred_element_type=F32)


def mm_tn(first, second):
    return lax.dot_general(first, second, (((0,), (0,)), ((), ())), preferred_element_type=F32)


def fold_rows(values):
    rows, width = values.shape
    return jnp.sum(values.reshape(rows // 8, 8, width), 0)


def gelu_pair(pre):
    below = 0.5 + 0.5 * lax.erf(pre * 0.7071067811865476)
    bell = jnp.exp2(pre * pre * (-0.5 * 1.4426950408889634))
    return pre * below, below + pre * bell * 0.3989422804014327


def const_spec(shape):
    zeros = (0,) * len(shape)
    return pl.BlockSpec(shape, lambda i, s: zeros, pipeline_mode=pl.Buffered(1))


def row_spec(block, width):
    return pl.BlockSpec((block, width), lambda i, s: (i, 0))


def params():
    return pltpu.CompilerParams(dimension_semantics=("arbitrary",), vmem_limit_bytes=VMEM_LIMIT)


def attn_fwd_kernel(block, rows, s_ref, x_ref, w_ref, b_ref, qkv_ref, p_ref, a_ref):
    cols = w_ref.shape[2]
    x = x_ref[...]
    q = ((mm(x, w_ref[0]) + b_ref[0:1, :]) * (HEAD_DIM**-0.5)).astype(LOW)
    k = mm(x, w_ref[1]).astype(LOW)
    v = (mm(x, w_ref[2]) + b_ref[1:2, :]).astype(LOW)
    qkv_ref[:, 0:cols] = q
    qkv_ref[:, cols : 2 * cols] = k
    qkv_ref[:, 2 * cols : 3 * cols] = v
    left = lax.broadcasted_iota(jnp.int32, (SEG, LANES), 1) < HEAD_DIM
    first_slot = s_ref[0] * rows + pl.program_id(0) * block
    zero = jnp.zeros((), LOW)
    for seg in range(block // SEG):
        at = slice(seg * SEG, (seg + 1) * SEG)
        slots = lax.broadcasted_iota(jnp.int32, (SEG, 2 * SEG), 0) + (first_slot + seg * SEG)
        bias = jnp.where(slots < s_ref[1], 0.0, -30000.0)
        for pair in range(cols // LANES):
            lanes = slice(pair * LANES, (pair + 1) * LANES)
            qp, kp, vp = q[at, lanes], k[at, lanes], v[at, lanes]
            both = jnp.concatenate([jnp.where(left, qp, zero), jnp.where(left, zero, qp)], 0)
            scores = mm_nt(kp, both) + bias
            top = jnp.max(scores, 0, keepdims=True)
            grown = jnp.exp(scores - top)
            probs = (grown * (1.0 / jnp.sum(grown, 0, keepdims=True))).astype(LOW)
            p_ref[at, 2 * pair * SEG : 2 * (pair + 1) * SEG] = probs
            stacked = jnp.concatenate([probs[:, :SEG], probs[:, SEG:]], 0)
            values = jnp.concatenate([jnp.where(left, vp, zero), jnp.where(left, zero, vp)], 0)
            a_ref[at, lanes] = mm_tn(stacked, values).astype(LOW)


def attn_fwd(scal, tokens, w, b, rows, block):
    cols = w.shape[2]
    width = tokens.shape[1]
    steps = rows // block
    heads = cols // HEAD_DIM
    return pl.pallas_call(
        functools.partial(attn_fwd_kernel, block, rows),
        grid_spec=pltpu.PrefetchScalarGridSpec(
            num_scalar_prefetch=1,
            grid=(steps,),
            in_specs=[
                pl.BlockSpec((block, width), lambda i, s: (s[0] * steps + i, 0)),
                const_spec(w.shape),
                const_spec(b.shape),
            ],
            out_specs=[row_spec(block, 3 * cols), row_spec(block, heads * SEG), row_spec(block, cols)],
        ),
        out_shape=[
            jax.ShapeDtypeStruct((rows, 3 * cols), LOW),
            jax.ShapeDtypeStruct((rows, heads * SEG), LOW),
            jax.ShapeDtypeStruct((rows, cols), LOW),
        ],
        compiler_params=params(),
        cost_estimate=pl.CostEstimate(
            flops=2 * rows * width * 3 * cols + 8 * rows * SEG * cols,
            bytes_accessed=rows * (width + 4 * cols + heads * SEG) * 2 + w.size * 2,
            transcendentals=rows * heads * SEG,
        ),
        name="attn_fwd",
    )(scal, tokens, w, b)


def spread(grad, out_ref, table, parts):
    if out_ref.shape[0] == 1:
        out_ref[0] = grad
        return
    share = grad.shape[0] // parts
    for part in range(parts):
        out_ref[table(part)] = grad[part * share : (part + 1) * share]


def slots_of(width, parts):
    share = width // parts
    return (parts, share) if share % 16 == 0 else (1, width)


def arrange(grad, table, parts):
    if grad.shape[0] == parts:
        return grad
    spots = jnp.zeros((parts,), jnp.int32).at[table].set(jnp.arange(parts, dtype=jnp.int32))
    return jnp.take(grad.reshape(parts, -1, grad.shape[2]), spots, axis=0)


class Fetch:
    def __init__(self, sources, targets, sems):
        self.copies = [pltpu.make_async_copy(s, t, sems.at[i]) for i, (s, t) in enumerate(zip(sources, targets))]

    def start(self):
        @pl.when(pl.program_id(0) == 0)
        def _():
            for copy in self.copies:
                copy.start()

    def wait(self, *which):
        @pl.when(pl.program_id(0) == 0)
        def _():
            for i in which:
                self.copies[i].wait()


ANY = pl.BlockSpec(memory_space=pl.ANY)


def ffn_fwd_kernel(
    block, rows, chunk, parts, steps,
    s_ref, x_ref, g_ref, ao_ref, at_ref, bu_ref, vec_ref, woo_hbm, wot_hbm, wuo_hbm, wut_hbm, wdo_hbm, wdt_hbm,
    gp_ref, low_ref, hat_ref, rs_ref, out_ref, own_ref, dmlp_ref, sums_ref, gt_ref, go_ref,
    woo_ref, wot_ref, wuo_ref, wut_ref, wdo_ref, wdt_ref, sems, hid_ref, all_ref,
):
    step = pl.program_id(0)
    half = wuo_ref.shape[1]
    fetch = Fetch(
        (woo_hbm, wot_hbm, wuo_hbm, wdo_hbm, wut_hbm, wdt_hbm),
        (woo_ref, wot_ref, wuo_ref, wdo_ref, wut_ref, wdt_ref),
        sems,
    )
    fetch.start()

    @pl.when(step == 0)
    def _():
        sums_ref[...] = jnp.zeros_like(sums_ref)

    @pl.when(step < steps)
    def _():
        b_out, gain_one, shift_one = vec_ref[0:1, :], vec_ref[1:2, :], vec_ref[2:3, :]
        b_down, gain_two, shift_two = vec_ref[3:4, :], vec_ref[4:5, :], vec_ref[5:6, :]
        fetch.wait(0, 1)
        h1 = x_ref[...].astype(F32) + mm(ao_ref[...], woo_ref[...]) + mm(at_ref[...], wot_ref[...]) + b_out
        center = h1 - jnp.mean(h1, -1, keepdims=True)
        scale = lax.rsqrt(jnp.mean(center * center, -1, keepdims=True) + EPS)
        hat = center * scale
        normed = hat * gain_one + shift_one
        hat_ref[...] = hat.astype(LOW)
        rs_ref[...] = jnp.broadcast_to(scale, rs_ref.shape)
        low = normed.astype(LOW)
        low_ref[...] = low
        total = normed + b_down
        mine = pl.ds(pl.multiple_of(step * block, block), block)
        for side, (wu, wd) in enumerate(((wuo_ref, wdo_ref), (wut_ref, wdt_ref))):
            fetch.wait(2 + 2 * side, 3 + 2 * side)
            for start in range(0, half, chunk):
                at = slice(start, start + chunk)
                where = slice(side * half + start, side * half + start + chunk)
                pre = mm(low, wu[:, at]) + bu_ref[:, where]
                hidden, slope = gelu_pair(pre)
                hidden = hidden.astype(LOW)
                hid_ref[mine, where] = hidden
                gp_ref[:, where] = slope.astype(LOW)
                total = total + mm(hidden, wd[at, :])
        center = total - jnp.mean(total, -1, keepdims=True)
        scale = lax.rsqrt(jnp.mean(center * center, -1, keepdims=True) + EPS)
        hat = center * scale
        result = hat * gain_two + shift_two
        out_ref[...] = result
        own_ref[...] = result.astype(own_ref.dtype)
        slots = lax.broadcasted_iota(jnp.int32, (block, 1), 0) + (s_ref[0] * rows + step * block)
        cot = jnp.where(slots < s_ref[1], g_ref[...], 0.0)
        inner = cot * gain_two
        d_h2 = scale * (
            inner - jnp.mean(inner, -1, keepdims=True) - hat * jnp.mean(inner * hat, -1, keepdims=True)
        )
        low = d_h2.astype(LOW)
        dmlp_ref[...] = low
        all_ref[mine, :] = low
        sums_ref[0:8, :] += fold_rows(cot * hat)
        sums_ref[8:16, :] += fold_rows(cot)
        sums_ref[16:24, :] += fold_rows(d_h2)

    wide = gt_ref.shape[2]
    for side, grad_ref in ((1, gt_ref), (0, go_ref)):
        for piece in range(half // wide):
            at = side * half + piece * wide

            @pl.when(step == steps + (1 - side) * (half // wide) + piece)
            def _():
                grad = mm_tn(all_ref[...], hid_ref[:, at : at + wide]).astype(LOW)
                spread(grad, grad_ref, lambda part: s_ref[2 + side * parts + part], parts)


def ffn_fwd(scal, tokens, grad_out, att, w_out, w_up, b_up, w_down, vec, rows, block, chunk, wide, parts):
    width = tokens.shape[1]
    steps = rows // block
    half = w_up[0].shape[1]
    pieces = half // wide
    cols = att[0].shape[1]
    last = steps - 1
    row = lambda i: jnp.minimum(i, last)
    mine = lambda i, s: (s[0] * steps + row(i), 0)
    rows_of = lambda w: pl.BlockSpec((block, w), lambda i, s: (row(i), 0))
    outs = [(2 * half, LOW), (width, LOW), (width, LOW), (LANES, F32)]
    lead = slots_of(width, parts)
    weights = [*w_out, *w_up, *w_down]
    grads = jax.ShapeDtypeStruct((*lead, half), LOW)
    clamp = lambda v: jnp.clip(v, 0, pieces - 1)
    return pl.pallas_call(
        functools.partial(ffn_fwd_kernel, block, rows, chunk, parts, steps),
        grid_spec=pltpu.PrefetchScalarGridSpec(
            num_scalar_prefetch=1,
            grid=(steps + 2 * pieces,),
            in_specs=[pl.BlockSpec((block, width), mine), pl.BlockSpec((block, width), mine), rows_of(cols), rows_of(cols)]
            + [const_spec(b_up.shape), const_spec(vec.shape)]
            + [ANY] * 6,
            out_specs=[rows_of(w) for w, _ in outs]
            + [pl.BlockSpec((block, width), mine), rows_of(width), rows_of(width)]
            + [pl.BlockSpec((24, width), lambda i, s: (0, 0))]
            + [
                pl.BlockSpec((*lead, wide), lambda i, s: (0, 0, clamp(i - steps))),
                pl.BlockSpec((*lead, wide), lambda i, s: (0, 0, clamp(i - steps - pieces))),
            ],
            scratch_shapes=[pltpu.VMEM(w.shape, LOW) for w in weights]
            + [pltpu.SemaphoreType.DMA((6,)), pltpu.VMEM((rows, 2 * half), LOW), pltpu.VMEM((rows, width), LOW)],
        ),
        out_shape=[jax.ShapeDtypeStruct((rows, w), t) for w, t in outs]
        + [
            jax.ShapeDtypeStruct((2 * rows, width), F32),
            jax.ShapeDtypeStruct((rows, width), OWN),
            jax.ShapeDtypeStruct((rows, width), LOW),
            jax.ShapeDtypeStruct((24, width), F32),
            grads,
            grads,
        ],
        compiler_params=params(),
        cost_estimate=pl.CostEstimate(
            flops=2 * rows * width * (6 * half + 2 * cols),
            bytes_accessed=rows * (4 * half + 24 * width),
            transcendentals=rows * 2 * half,
        ),
        name="ffn_fwd",
    )(scal, tokens, grad_out, *att, b_up, vec, *weights)


def ffn_bwd_kernel(
    block, chunk, parts, steps,
    s_ref, dmlp_ref, gp_ref, hat_ref, rs_ref, low_ref, ao_ref, at_ref, vec_ref,
    woo_hbm, wot_hbm, wuo_hbm, wut_hbm, wdo_hbm, wdt_hbm,
    dh1_ref, dao_ref, dat_ref, sums_ref, bup_ref, gt_ref, go_ref, ot_ref, oo_ref,
    woo_ref, wot_ref, wuo_ref, wut_ref, wdo_ref, wdt_ref, sems, dpre_ref, dbr_ref,
):
    step = pl.program_id(0)
    half = wuo_ref.shape[1]
    fetch = Fetch(
        (wdo_hbm, wuo_hbm, wdt_hbm, wut_hbm, woo_hbm, wot_hbm),
        (wdo_ref, wuo_ref, wdt_ref, wut_ref, woo_ref, wot_ref),
        sems,
    )
    fetch.start()

    @pl.when(step == 0)
    def _():
        sums_ref[...] = jnp.zeros_like(sums_ref)
        bup_ref[...] = jnp.zeros_like(bup_ref)

    @pl.when(step < steps)
    def _():
        mine = pl.ds(pl.multiple_of(step * block, block), block)
        d_mlp = dmlp_ref[...]
        total = d_mlp.astype(F32)
        for side, (wu, wd) in enumerate(((wuo_ref, wdo_ref), (wut_ref, wdt_ref))):
            fetch.wait(2 * side, 2 * side + 1)
            for start in range(0, half, chunk):
                at = slice(start, start + chunk)
                where = slice(side * half + start, side * half + start + chunk)
                d_hidden = mm_nt(d_mlp, wd[at, :])
                d_pre = (d_hidden * gp_ref[:, where].astype(F32)).astype(LOW)
                dpre_ref[mine, where] = d_pre
                bup_ref[:, where] += fold_rows(d_pre.astype(F32))
                total = total + mm_nt(d_pre, wu[:, at])
        hat = hat_ref[...].astype(F32)
        inner = total * vec_ref[1:2, :]
        scale = rs_ref[:, 0:1]
        d_h1 = scale * (
            inner - jnp.mean(inner, -1, keepdims=True) - hat * jnp.mean(inner * hat, -1, keepdims=True)
        )
        sums_ref[0:8, :] += fold_rows(total * hat)
        sums_ref[8:16, :] += fold_rows(total)
        sums_ref[16:24, :] += fold_rows(d_h1)
        dh1_ref[...] = d_h1
        low = d_h1.astype(LOW)
        dbr_ref[mine, :] = low
        fetch.wait(4, 5)
        dao_ref[...] = mm_nt(low, woo_ref[...]).astype(LOW)
        dat_ref[...] = mm_nt(low, wot_ref[...]).astype(LOW)

    wide = gt_ref.shape[2]
    pieces = half // wide
    for side, grad_ref in ((1, gt_ref), (0, go_ref)):
        for piece in range(pieces):
            at = side * half + piece * wide

            @pl.when(step == steps + (1 - side) * pieces + piece)
            def _():
                grad = mm_tn(low_ref[...], dpre_ref[:, at : at + wide]).astype(LOW)
                spread(grad, grad_ref, lambda part: s_ref[2 + side * parts + part], parts)

    @pl.when(step == steps + 2 * pieces)
    def _():
        for side, (att_ref, grad_ref) in enumerate(((ao_ref, oo_ref), (at_ref, ot_ref))):
            grad = mm_tn(dbr_ref[...], att_ref[...]).astype(LOW)
            spread(grad, grad_ref, lambda part: s_ref[2 + side * parts + part], parts)


def ffn_bwd(scal, d_mlp, slope, hat, scale, normed_low, att, w_out, w_up, w_down, vec, block, chunk, wide, parts):
    rows, width = d_mlp.shape
    steps = rows // block
    half = w_up[0].shape[1]
    pieces = half // wide
    cols = w_out[0].shape[0]
    last = steps - 1
    rows_of = lambda w: pl.BlockSpec((block, w), lambda i, s: (jnp.minimum(i, last), 0))
    fixed = lambda shape: pl.BlockSpec(shape, lambda i, s: (0,) * len(shape))
    moving = [d_mlp, slope, hat, scale]
    consts = [normed_low, *att, vec]
    weights = [*w_out, *w_up, *w_down]
    outs = [(width, F32), (cols, LOW), (cols, LOW)]
    lead = slots_of(width, parts)
    grads = jax.ShapeDtypeStruct((*lead, half), LOW)
    narrow = jax.ShapeDtypeStruct((*lead, cols), LOW)
    clamp = lambda v: jnp.clip(v, 0, pieces - 1)
    return pl.pallas_call(
        functools.partial(ffn_bwd_kernel, block, chunk, parts, steps),
        grid_spec=pltpu.PrefetchScalarGridSpec(
            num_scalar_prefetch=1,
            grid=(steps + 2 * pieces + 1,),
            in_specs=[rows_of(m.shape[1]) for m in moving] + [const_spec(c.shape) for c in consts] + [ANY] * 6,
            out_specs=[rows_of(w) for w, _ in outs]
            + [fixed((24, width)), fixed((8, 2 * half))]
            + [
                pl.BlockSpec((*lead, wide), lambda i, s: (0, 0, clamp(i - steps))),
                pl.BlockSpec((*lead, wide), lambda i, s: (0, 0, clamp(i - steps - pieces))),
                fixed((*lead, cols)),
                fixed((*lead, cols)),
            ],
            scratch_shapes=[pltpu.VMEM(w.shape, LOW) for w in weights]
            + [pltpu.SemaphoreType.DMA((6,)), pltpu.VMEM((rows, 2 * half), LOW), pltpu.VMEM((rows, width), LOW)],
        ),
        out_shape=[jax.ShapeDtypeStruct((rows, w), t) for w, t in outs]
        + [jax.ShapeDtypeStruct((24, width), F32), jax.ShapeDtypeStruct((8, 2 * half), F32), grads, grads, narrow, narrow],
        compiler_params=params(),
        cost_estimate=pl.CostEstimate(
            flops=2 * rows * width * (6 * half + 4 * cols),
            bytes_accessed=rows * (4 * half + 20 * width),
            transcendentals=0,
        ),
        name="ffn_bwd",
    )(scal, *moving, *consts, *weights)


def attn_bwd_kernel(block, side, parts, steps, s_ref, x_ref, qkv_ref, p_ref, da_ref, dl_ref, sums_ref, grad_ref, all_ref):
    cols = da_ref.shape[1]
    step = pl.program_id(0)

    @pl.when(step == 0)
    def _():
        sums_ref[...] = jnp.zeros_like(sums_ref)

    left = lax.broadcasted_iota(jnp.int32, (SEG, LANES), 1) < HEAD_DIM
    zero = jnp.zeros((), LOW)

    def split(values):
        return jnp.concatenate([jnp.where(left, values, zero), jnp.where(left, zero, values)], 0)

    @pl.when(step < steps)
    def _():
        for pair in range(cols // LANES):
            lanes = slice(pair * LANES, (pair + 1) * LANES)
            k_lanes = slice(cols + pair * LANES, cols + (pair + 1) * LANES)
            v_lanes = slice(2 * cols + pair * LANES, 2 * cols + (pair + 1) * LANES)
            sum_q = jnp.zeros((8, LANES), F32)
            sum_v = jnp.zeros((8, LANES), F32)
            for seg in range(block // SEG):
                at = slice(seg * SEG, (seg + 1) * SEG)
                qp, kp, vp, dap = qkv_ref[at, lanes], qkv_ref[at, k_lanes], qkv_ref[at, v_lanes], da_ref[at, lanes]
                probs = p_ref[at, 2 * pair * SEG : 2 * (pair + 1) * SEG]
                da_split = split(dap)
                d_probs = mm_nt(vp, da_split)
                wide = probs.astype(F32)
                d_scores = (wide * (d_probs - jnp.sum(wide * d_probs, 0, keepdims=True))).astype(LOW)
                d_v = mm(probs, da_split).astype(LOW)
                d_k = mm(d_scores, split(qp)).astype(LOW)
                stacked = jnp.concatenate([d_scores[:, :SEG], d_scores[:, SEG:]], 0)
                d_q = (mm_tn(stacked, split(kp)) * (HEAD_DIM**-0.5)).astype(LOW)
                dl_ref[at, lanes] = d_q
                dl_ref[at, k_lanes] = d_k
                dl_ref[at, v_lanes] = d_v
                sum_q += fold_rows(d_q.astype(F32))
                sum_v += fold_rows(d_v.astype(F32))
            sums_ref[:, lanes] += sum_q
            sums_ref[:, k_lanes] += sum_v
        all_ref[pl.ds(pl.multiple_of(step * block, block), block), :] = dl_ref[...]

    wide = grad_ref.shape[2]
    for piece in range(3 * cols // wide):

        @pl.when(step == steps + piece)
        def _():
            grad = mm_tn(x_ref[...], all_ref[:, piece * wide : (piece + 1) * wide]).astype(LOW)
            spread(grad, grad_ref, lambda part: s_ref[2 + side * parts + part], parts)


def attn_bwd(scal, tokens, qkv, probs, d_att, side, block, wide, parts):
    rows, cols = d_att.shape
    width = tokens.shape[1]
    steps = rows // block
    pieces = 3 * cols // wide
    last = steps - 1
    rows_of = lambda w: pl.BlockSpec((block, w), lambda i, s: (jnp.minimum(i, last), 0))
    moving = [qkv, probs, d_att]
    lead = slots_of(width, parts)
    return pl.pallas_call(
        functools.partial(attn_bwd_kernel, block, side, parts, steps),
        grid_spec=pltpu.PrefetchScalarGridSpec(
            num_scalar_prefetch=1,
            grid=(steps + pieces,),
            in_specs=[pl.BlockSpec((rows, width), lambda i, s: (s[0], 0), pipeline_mode=pl.Buffered(1))]
            + [rows_of(m.shape[1]) for m in moving],
            out_specs=[
                rows_of(3 * cols),
                pl.BlockSpec((8, 2 * cols), lambda i, s: (0, 0)),
                pl.BlockSpec((*lead, wide), lambda i, s: (0, 0, jnp.clip(i - steps, 0, pieces - 1))),
            ],
            scratch_shapes=[pltpu.VMEM((rows, 3 * cols), LOW)],
        ),
        out_shape=[
            jax.ShapeDtypeStruct((rows, 3 * cols), LOW),
            jax.ShapeDtypeStruct((8, 2 * cols), F32),
            jax.ShapeDtypeStruct((*lead, 3 * cols), LOW),
        ],
        compiler_params=params(),
        cost_estimate=pl.CostEstimate(
            flops=16 * rows * SEG * cols * 2 + 6 * rows * width * cols,
            bytes_accessed=rows * (7 * cols + probs.shape[1]) * 2,
            transcendentals=0,
        ),
        name="attn_bwd",
    )(scal, tokens, *moving)


def d_tokens_kernel(s_ref, dh1_ref, dlo_ref, dlt_ref, wo_ref, wt_ref, out_ref, own_ref):
    cols = wo_ref.shape[2]
    total = dh1_ref[...]
    for d_lin, w in ((dlo_ref, wo_ref), (dlt_ref, wt_ref)):
        for kind in range(3):
            total = total + mm_nt(d_lin[:, kind * cols : (kind + 1) * cols], w[kind])
    out_ref[...] = total
    own_ref[...] = total


def d_tokens_of(scal, d_h1, d_lin, w_qkv, block):
    rows, width = d_h1.shape
    steps = rows // block
    wide = d_lin[0].shape[1]
    return pl.pallas_call(
        d_tokens_kernel,
        grid_spec=pltpu.PrefetchScalarGridSpec(
            num_scalar_prefetch=1,
            grid=(steps,),
            in_specs=[row_spec(block, width), row_spec(block, wide), row_spec(block, wide)]
            + [const_spec(w.shape) for w in w_qkv],
            out_specs=[pl.BlockSpec((block, width), lambda i, s: (s[0] * steps + i, 0)), row_spec(block, width)],
        ),
        out_shape=[jax.ShapeDtypeStruct((2 * rows, width), F32), jax.ShapeDtypeStruct((rows, width), F32)],
        compiler_params=params(),
        cost_estimate=pl.CostEstimate(
            flops=4 * rows * width * wide, bytes_accessed=rows * (12 * width + 4 * wide), transcendentals=0
        ),
        name="d_tokens",
    )(scal, d_h1, *d_lin, *w_qkv)


def place_kernel(s_ref, whole_ref, part_ref, out_ref):
    out_ref[...] = part_ref[...]


def place_other(scal, whole, part, block):
    rows, width = part.shape
    steps = rows // block
    return pl.pallas_call(
        place_kernel,
        grid_spec=pltpu.PrefetchScalarGridSpec(
            num_scalar_prefetch=1,
            grid=(steps,),
            in_specs=[pl.BlockSpec(memory_space=pl.ANY), row_spec(block, width)],
            out_specs=pl.BlockSpec((block, width), lambda i, s: ((1 - s[0]) * steps + i, 0)),
        ),
        out_shape=jax.ShapeDtypeStruct(whole.shape, F32),
        input_output_aliases={1: 0},
        compiler_params=params(),
        cost_estimate=pl.CostEstimate(flops=0, bytes_accessed=8 * rows * width, transcendentals=0),
        name="place_other",
    )(scal, whole, part)


def shards(
    n_docs, tokens, grad_out, live_tokens, w_qkv, b_qv, w_out, b_out, gain_one, shift_one, w_up, b_up, w_down, b_down,
    gain_two, shift_two,
):
    c = lax.axis_index("heads")
    me = lax.axis_index("docs")
    rows = tokens.shape[0] // 2
    bits = n_docs.bit_length() - 1
    orders = [list(range(bits)), [1, 0] + list(range(2, bits))]

    def step_pairs(stage):
        return [
            (d * 2 + h, (d ^ (1 << orders[h][stage])) * 2 + h) for d in range(n_docs) for h in range(2)
        ]

    def step(value, stage):
        return lax.ppermute(value, ("docs", "heads"), step_pairs(stage))

    def swap(value):
        return lax.ppermute(value, "heads", [(0, 1), (1, 0)])

    def table_for(core):
        away = jnp.arange(n_docs, dtype=jnp.int32) ^ me
        slots = []
        for order in orders:
            slot = jnp.zeros((n_docs,), jnp.int32)
            for place, bit in enumerate(order):
                slot = slot | (((away >> bit) & 1) << (bits - 1 - place))
            slots.append(slot)
        return jnp.where(core == 0, slots[0], slots[1])

    tables = (table_for(c), table_for(1 - c))
    scal = jnp.concatenate([c[None].astype(jnp.int32), live_tokens, *tables])

    w_qkv = jnp.transpose(w_qkv, (1, 0, 2))
    w_qkv2 = (w_qkv, swap(w_qkv))
    b_qv2 = (b_qv, swap(b_qv))
    w_out2 = (w_out, swap(w_out))
    w_up2 = (w_up, swap(w_up))
    w_down2 = (w_down, swap(w_down))
    b_up2 = jnp.concatenate([b_up, swap(b_up)])[None]
    vec = jnp.stack([b_out, gain_one, shift_one, b_down, gain_two, shift_two, b_out, b_out])

    def add(left, right):
        return (left.astype(F32) + right.astype(F32)).astype(LOW)

    def first_sum(pairs):
        half = n_docs // 2
        parts = [(arrange(own, tables[0], n_docs), arrange(swap(other), tables[0], n_docs)) for own, other in pairs]
        cut = lambda at: jnp.concatenate([add(own[at], other[at]) for own, other in parts], 2)
        return cut(slice(half, None)), cut(slice(None, half))

    def next_sum(keep, came):
        half = keep.shape[0] // 2
        if not half:
            return (keep.astype(F32) + came.astype(F32))[0]
        return add(keep[half:], came[half:]), add(keep[:half], came[:half])

    def after(value, *before):
        return lax.optimization_barrier((value, *before))[0]

    block = 256
    qkv, probs, att = [None] * 2, [None] * 2, [None] * 2
    for side in range(2):
        qkv[side], probs[side], att[side] = attn_fwd(scal, tokens, w_qkv2[side], b_qv2[side], rows, block)
    half = w_up.shape[1]
    slope, normed_low, hat, scale, layer_out, layer_own, d_mlp, sums_two, down_other, down_own = ffn_fwd(
        scal, tokens, grad_out, att, w_out2, w_up2, b_up2, w_down2, vec, rows, block, BWD_CHUNK, 768, n_docs
    )
    layer_out = place_other(scal, layer_out, swap(layer_own), block)
    send, keep = first_sum([(down_own, down_other)])
    down = [(send, keep)]
    came_down = step(send, 0)
    d_mlp = after(d_mlp, send)
    d_h1, d_att_own, d_att_other, sums_one, sums_up, up_other, up_own, out_other, out_own = ffn_bwd(
        scal, d_mlp, slope, hat, scale, normed_low, att, w_out2, w_up2, w_down2, vec, block, BWD_CHUNK, 768, n_docs
    )

    def run(send, keep, came=None):
        for stage in range(bits):
            if came is None:
                came = step(send, stage)
            if stage == bits - 1:
                return next_sum(keep, came)
            send, keep = next_sum(keep, came)
            came = None

    d_w_down = run(send, keep, came_down).T
    up = first_sum([(up_own, up_other), (out_own, out_other)])
    d_att_other = after(d_att_other, up[0])
    rest = run(*up)
    d_w_up, d_w_out = rest[:, :half], rest[:, half:].T
    cols = att[0].shape[1]
    d_lin_other, sums_other, lin_other = attn_bwd(scal, tokens, qkv[1], probs[1], d_att_other, 1, block, cols, n_docs)
    d_lin_own, sums_own, lin_own = attn_bwd(scal, tokens, qkv[0], probs[0], d_att_own, 0, block, cols, n_docs)
    lin = first_sum([(lin_own, lin_other)])
    d_w_qkv = run(*lin)
    d_h1 = after(d_h1, lin[0])
    d_tokens, d_tok_own = d_tokens_of(scal, d_h1, (d_lin_own, d_lin_other), w_qkv2, block)
    d_tokens = place_other(scal, d_tokens, swap(d_tok_own), block)

    width = tokens.shape[1]
    common = jnp.concatenate([jnp.sum(s.reshape(3, 8, width), 1).reshape(-1) for s in (sums_two, sums_one)])
    sums_up = jnp.sum(sums_up, 0)
    other = jnp.concatenate([sums_up[half:], jnp.sum(sums_other, 0)])
    own = jnp.concatenate([sums_up[:half], jnp.sum(sums_own, 0)])
    small = jnp.concatenate([common, own]) + swap(jnp.concatenate([common, other]))
    small = small.reshape(-1, LANES)
    for stage in range(bits):
        small = small + lax.ppermute(small, "docs", [(d, d ^ (1 << stage)) for d in range(n_docs)])
    small = small.reshape(-1)
    d_gain_two, d_shift_two, d_b_down, d_gain_one, d_shift_one, d_b_out = small[: 6 * width].reshape(6, width)
    d_b_up = small[6 * width : 6 * width + half]
    d_b_qv = small[6 * width + half :].reshape(2, cols)
    return (
        layer_out,
        d_tokens,
        jnp.transpose(d_w_qkv.reshape(-1, 3, cols), (0, 1, 2)),
        d_b_qv,
        d_w_out,
        d_b_out,
        d_gain_one,
        d_shift_one,
        d_w_up,
        d_b_up,
        d_w_down,
        d_b_down,
        d_gain_two,
        d_shift_two,
    )


def solution(mesh):
    placed = (
        P("docs", None),
        P("docs", None),
        P("docs"),
        P(None, None, "heads"),
        P(None, "heads"),
        P("heads", None),
        P(),
        P(),
        P(),
        P(None, "heads"),
        P("heads"),
        P("heads", None),
        P(),
        P(),
        P(),
    )
    return jax.shard_map(
        functools.partial(shards, mesh.shape["docs"]),
        mesh=mesh,
        in_specs=placed,
        out_specs=(
            P("docs", None),
            P("docs", None),
            P("docs", None, "heads"),
            P(None, "heads"),
            P("heads", "docs"),
            P(),
            P(),
            P(),
            P("docs", "heads"),
            P("heads"),
            P("heads", "docs"),
            P(),
            P(),
            P(),
        ),
        check_vma=False,
    )
```

time: 866 us -> 236 us (0.27)
  waiting for transfers between devices: 512 us -> 33.8 us
  Pallas kernels: 0 us -> 131 us
  matrix products: 115 us -> 0 us
  blocking collectives: 77.7 us -> 0 us
  local copies, waits for them, and re-layouts: 82.7 us -> 10.3 us
  starting transfers between devices: 0.58 us -> 32.3 us
  other arithmetic: 54.4 us -> 26.1 us
  between operations: 15.9 us -> 1.67 us
    reduce_scatter x4 -> x0, waiting for transfers between devices: 437 us -> none  [the longest x1 142 us: shards(): lax.psum_scatter(d_w_up, 'docs', scatter_dimension=0, tiled=True)]
    pallas_call x0 -> x9, Pallas kernels: none -> 131 us  [the longest x1 34 us: ffn_fwd(): pl.pallas_call(functools.partial(ffn_fwd_kernel, block, rows, chunk, part...]
    dot_general x18 -> x0, matrix products: 115 us -> none  [the longest x4 40.7 us: left_dot(): lax.dot_general(first, second, (((0,), (0,)), ((), ())), preferred_elemen...]
    psum x1 -> x0, blocking collectives: 77.7 us -> none  [shards(): lax.psum((d_b_qv, d_b_out, d_gain_one, d_shift_one, d_b_up, d_b_down, d_g...]
    psum x4 -> x0, waiting for transfers between devices: 74.9 us -> none  [the longest x1 26 us: shards(): lax.psum(attn_part.astype(jnp.bfloat16), 'heads').astype(jnp.float32)]
    reduce_sum x11 -> x5, other arithmetic: 46.1 us -> 5.15 us  [the longest x2 2.14 us: shards(): jnp.sum(s.reshape(3, 8, width), 1).reshape(-1)]
    ppermute x0 -> x29, waiting for transfers between devices: none -> 33.8 us  [the longest x12 23.4 us: step(): return lax.ppermute(value, ('docs', 'heads'), step_pairs(stage))]
    ppermute x0 -> x29, starting transfers between devices: none -> 32.3 us  [the longest x12 18.8 us: step(): return lax.ppermute(value, ('docs', 'heads'), step_pairs(stage))]
  transfers between devices with their start and end apart: 8 -> 29, of which waited for: 7 -> 9; matrix products, arithmetic and copies ran while one was open for 7% -> 13% of each run, Pallas kernels for 0% -> 25%
where the time goes in v1:
time: 236 us; the launch traced here: 235 us
  Pallas kernels  131 us (56%)
  waiting for transfers between devices  33.8 us (14%)
  starting transfers between devices  32.3 us (14%)
  other arithmetic  26.1 us (11%)
  local copies, waits for them, and re-layouts  10.3 us (4%)
    pallas_call x1, Pallas kernels, ffn_fwd(): pl.pallas_call(functools.partial(ffn_fwd_kernel, block, rows, chunk, part...  34 us
    pallas_call x1, Pallas kernels, ffn_bwd(): pl.pallas_call(functools.partial(ffn_bwd_kernel, block, chunk, parts, ste...  32.7 us
    pallas_call x2, Pallas kernels, attn_bwd(): pl.pallas_call(functools.partial(attn_bwd_kernel, block, side, parts, ste...  26.5 us
    ppermute x12, waiting for transfers between devices, step(): return lax.ppermute(value, ('docs', 'heads'), step_pairs(stage))  23.4 us
    ppermute x12, starting transfers between devices, step(): return lax.ppermute(value, ('docs', 'heads'), step_pairs(stage))  18.8 us
    pallas_call x2, Pallas kernels, attn_fwd(): pl.pallas_call(functools.partial(attn_fwd_kernel, block, rows), grid_spec...  16.6 us
    convert_element_type x13, other arithmetic, add(): return (left.astype(F32) + right.astype(F32)).astype(LOW)  16.4 us
    pallas_call x1, Pallas kernels, d_tokens_of(): pl.pallas_call(d_tokens_kernel, grid_spec=pltpu.PrefetchScalarGridSpec(nu...  11 us
  transfers between devices with their start and end apart: 29, of which 9 were waited for; matrix products, arithmetic and copies ran while one was open for 13% of the time, Pallas kernels for 25%

profile of v1, /device:TPU:0, one launch (start us, length us, event | category | flops | bytes accessed | tf_op | source)
XLA Modules:
  0.0 234.8 jit_solution(11604191809853919897)
XLA Ops:
  3.6 8.3 %attn_fwd.2 = (bf16[1024,1152]{1,0:T(8,128)(2,1)}, bf16[1024,768]{1,0:T(8,128)(2,1)}, bf16[1024,384]{1,0:T(8,128)(2,1)}) custom-call(s32[34]{0:T(128)} %pad_add_fusion.s_ref, bf16[2048,768]{1,0:T(8,128)(2,1)} %x_ref.9, bf16[3,768,384]{2,1,0:T(8,128)(2,1)} %bitcast.37, f32[2,384]{1,0:T(2,128)} %b_ref.1), custom_call_target="tpu_custom_call" | custom-call | flops 2214592512 | bytes 8060928 | tf_op jit(solution)/shard_map/attn_fwd/pallas_call | solution.py:92
  14.4 8.3 %attn_fwd.3 = (bf16[1024,1152]{1,0:T(8,128)(2,1)}, bf16[1024,768]{1,0:T(8,128)(2,1)}, bf16[1024,384]{1,0:T(8,128)(2,1)}) custom-call(s32[34]{0:T(128)} %pad_add_fusion.s_ref, bf16[2048,768]{1,0:T(8,128)(2,1)} %x_ref.9, bf16[3,768,384]{2,1,0:T(8,128)(2,1)} %collective-permute-done.w_ref.wt_ref, f32[2,384]{1,0:T(2,128)} %copy-done.17), custom_call_target="tpu_custom_call" | custom-call | flops 2214592512 | bytes 8060928 | tf_op jit(solution)/shard_map/attn_fwd/pallas_call | solution.py:92
  24.4 34.0 %ffn_fwd.1 = (bf16[1024,3072]{1,0:T(8,128)(2,1)}, bf16[1024,768]{1,0:T(8,128)(2,1)}, bf16[1024,768]{1,0:T(8,128)(2,1)}, f32[1024,128]{1,0:T(8,128)}, f32[2048,76...) custom-call(s32[34]{0:T(128)} %pad_add_fusion.s_ref, ...), custom_call_target="tpu_custom_call" | custom-call | flops 15703474176 | bytes 25165824 | tf_op jit(solution)/shard_map/ffn_fwd/pallas_call | solution.py:251
  58.6 4.6 %collective-permute-done.7 = bf16[16,48,1536]{2,1,0:T(8,128)(2,1)S(1)} collective-permute-done((bf16[16,48,1536]{2,1,0:T(8,128)(2,1)}, bf16[16,48,1536]{2,1,0:T(8,128)(2,1)S(1)}, u32[]{:S(2)}, u32[]{:S(2)}) %collective-permute-start.7) | collective-permute-done | bytes 2359328 | tf_op jit(solution)/shard_map/ppermute | solution.py:568
  63.1 3.4 %add_convert_fusion = (bf16[8,48,1536]{2,1,0:T(8,128)(2,1)S(1)}, bf16[8,48,1536]{2,1,0:T(8,128)(2,1)}) fusion(bf16[16,48,1536]{2,1,0:T(8,128)(2,1)S(1)} %collective-permute-done.7, bf16[16,48,1536]{2,1,0:T(8,128)(2,1)} %get-tuple-element.55), kind=kLoop, calls=%fused_computation | loop fusion | flops 4718592 | bytes 7077888 | tf_op jit(solution)/shard_map/convert_element_type | solution.py:593
  66.5 32.7 %ffn_bwd.1 = (f32[1024,768]{1,0:T(8,128)}, bf16[1024,384]{1,0:T(8,128)(2,1)}, bf16[1024,384]{1,0:T(8,128)(2,1)}, f32[24,768]{1,0:T(8,128)}, f32[8,3072]{1,0:T(8,...) custom-call(s32[34]{0:T(128)} %pad_add_fusion.s_ref, ...), custom_call_target="tpu_custom_call" | custom-call | flops 16911433728 | bytes 22020096 | tf_op jit(solution)/shard_map/ffn_bwd/pallas_call | solution.py:375
  99.4 2.8 %collective-permute-start.25 = (bf16[8,48,1536]{2,1,0:T(8,128)(2,1)}, bf16[8,48,1536]{2,1,0:T(8,128)(2,1)}, u32[]{:S(2)}, u32[]{:S(2)}) collective-permute-start(bf16[8,48,1536]{2,1,0:T(8,128)(2,1)} %get-tuple-element.115), channel_id=1, source_target_pairs={{0,2},{1,5},{2,0},{3,7},{4,6},{5,1},{6,4},{7,3},{8,10},{9,13},{10,... | collective-permute-start | bytes 3538952 | tf_op jit(solution)/shard_map/ppermute | solution.py:565
  108.4 13.3 %attn_bwd.2 = (bf16[1024,1152]{1,0:T(8,128)(2,1)}, f32[8,768]{1,0:T(8,128)}, bf16[16,48,1152]{2,1,0:T(8,128)(2,1)}) custom-call(s32[34]{0:T(128)} %pad_add_fusion.s_ref, bf16[2048,768]{1,0:T(8,128)(2,1)} %x_ref.9, bf16[1024,1152]{1,0:T(8,128)(2,1)} %get-tuple-element.63.qkv_ref, bf16[1024,768]{1,0:T(8,128)(2,1)} %get-tuple-element.64.p_ref, ...), custom_call_target="tpu_custom_call" | custom-call | flops 3422552064 | bytes 7077888 | tf_op jit(solution)/shard_map/attn_bwd/pallas_call | solution.py:465
  123.8 2.1 add_convert_fusion.16
  125.9 2.8 %add_convert_fusion.9 = (bf16[4,48,1536]{2,1,0:T(8,128)(2,1)}, bf16[4,48,1536]{2,1,0:T(8,128)(2,1)}) fusion(bf16[8,48,1536]{2,1,0:T(8,128)(2,1)} %collective-permute-done.25, bf16[8,48,1536]{2,1,0:T(8,128)(2,1)S(1)} %get-tuple-element.114), kind=kLoop, calls=%fused_computation.12 | loop fusion | flops 2359296 | bytes 3538944 | tf_op jit(solution)/shard_map/convert_element_type | solution.py:593
  131.1 13.2 %attn_bwd.3 = (bf16[1024,1152]{1,0:T(8,128)(2,1)}, f32[8,768]{1,0:T(8,128)}, bf16[16,48,1152]{2,1,0:T(8,128)(2,1)}) custom-call(s32[34]{0:T(128)} %pad_add_fusion.s_ref, bf16[2048,768]{1,0:T(8,128)(2,1)} %x_ref.9, bf16[1024,1152]{1,0:T(8,128)(2,1)} %get-tuple-element.67.qkv_ref, bf16[1024,768]{1,0:T(8,128)(2,1)} %get-tuple-element.68.p_ref, ...), custom_call_target="tpu_custom_call" | custom-call | flops 3422552064 | bytes 7077888 | tf_op jit(solution)/shard_map/attn_bwd/pallas_call | solution.py:465
  150.9 1.8 collective-permute-done.17
  154.0 1.8 collective-permute-done.27
  155.9 2.7 %collective-permute-start.28 = (bf16[1,48,1536]{2,1,0:T(8,128)(2,1)S(1)}, bf16[1,48,1536]{2,1,0:T(8,128)(2,1)S(1)}, u32[]{:S(2)}, u32[]{:S(2)}) collective-permute-start(bf16[1,48,1536]{2,1,0:T(8,128)(2,1)S(1)} %add_convert_fusion.22), channel_id=1, source_target_pairs={{0,16},{1,17},{2,18},{3,19},{4,20},{5,21},{6,22},{7,23},{8,24},{9,... | collective-permute-start | bytes 442376 | tf_op jit(solution)/shard_map/ppermute | solution.py:565
  160.9 5.0 %place_other.2 = f32[2048,768]{1,0:T(8,128)} custom-call(s32[34]{0:T(128)} %pad_add_fusion.s_ref, f32[2048,768]{1,0:T(8,128)} %get-tuple-element.52.whole_ref, f32[1024,768]{1,0:T(8,128)} %collective-permute-done.6.part_ref), custom_call_target="tpu_custom_call", output_to_operand_aliasing={{}: (1, {})} | custom-call | bytes 6291456 | tf_op jit(solution)/shard_map/place_other/pallas_call | solution.py:533
  167.4 3.5 %collective-permute-done.20 = f32[54,128]{1,0:T(8,128)S(1)} collective-permute-done((f32[54,128]{1,0:T(8,128)S(1)}, f32[54,128]{1,0:T(8,128)S(1)}, u32[]{:S(2)}, u32[]{:S(2)}) %collective-permute-start.20) | collective-permute-done | bytes 27680 | tf_op jit(solution)/shard_map/ppermute | solution.py:658
  174.0 2.8 %add_convert_fusion.4 = (bf16[8,48,1152]{2,1,0:T(8,128)(2,1)S(1)}, bf16[8,48,1152]{2,1,0:T(8,128)(2,1)}) fusion(bf16[16,48,1152]{2,1,0:T(8,128)(2,1)} %collective-permute-done.10, bf16[16,48,1152]{2,1,0:T(8,128)(2,1)S(1)} %copy-done.2), kind=kLoop, calls=%fused_computation.4 | loop fusion | flops 3538944 | bytes 5308416 | tf_op jit(solution)/shard_map/convert_element_type | solution.py:593
  178.9 11.0 %d_tokens.1 = (f32[2048,768]{1,0:T(8,128)}, f32[1024,768]{1,0:T(8,128)}) custom-call(s32[34]{0:T(128)} %pad_add_fusion.s_ref, f32[1024,768]{1,0:T(8,128)} %get-tuple-element.76.dh1_ref, bf16[1024,1152]{1,0:T(8,128)(2,1)} %get-tuple-element.77.dlo_ref, bf16[1024,1152]{1,0:T(8,128)(2,1)} %get-tuple-element.78.dlt_ref, bf16[3,768,384]{2,1,0:T(8,128)(2,1)} %bitcast.38, ...), custom_call_target="tpu_custom_call" | custom-call | flops 3623878656 | bytes 14155776 | tf_op jit(solution)/shard_map/d_tokens/pallas_call | solution.py:508
  189.9 7.3 %collective-permute-start.11 = (f32[1024,768]{1,0:T(8,128)}, f32[1024,768]{1,0:T(8,128)}, u32[]{:S(2)}, u32[]{:S(2)}) collective-permute-start(f32[1024,768]{1,0:T(8,128)} %get-tuple-element.80), channel_id=1, source_target_pairs={{0,1},{1,0},{2,3},{3,2},{4,5},{5,4},{6,7},{7,6},{8,9},{9,8},{10,11... | collective-permute-start | bytes 9437192 | tf_op jit(solution)/shard_map/ppermute | solution.py:568
  201.9 7.8 %collective-permute-done.23 = bf16[2,48,1920]{2,1,0:T(8,128)(2,1)S(1)} collective-permute-done((bf16[2,48,1920]{2,1,0:T(8,128)(2,1)S(1)}, bf16[2,48,1920]{2,1,0:T(8,128)(2,1)S(1)}, u32[]{:S(2)}, u32[]{:S(2)}) %collective-permute-start.23) | collective-permute-done | bytes 368672 | tf_op jit(solution)/shard_map/ppermute | solution.py:565
  209.8 2.0 collective-permute-start.24
  213.7 7.3 %collective-permute-done.24 = bf16[1,48,1920]{2,1,0:T(8,128)(2,1)S(1)} collective-permute-done((bf16[1,48,1920]{2,1,0:T(8,128)(2,1)S(1)}, bf16[1,48,1920]{2,1,0:T(8,128)(2,1)S(1)}, u32[]{:S(2)}, u32[]{:S(2)}) %collective-permute-start.24) | collective-permute-done | bytes 184352 | tf_op jit(solution)/shard_map/ppermute | solution.py:565
  223.7 5.3 %collective-permute-done.15 = bf16[1,48,1152]{2,1,0:T(8,128)(2,1)S(1)} collective-permute-done((bf16[1,48,1152]{2,1,0:T(8,128)(2,1)S(1)}, bf16[1,48,1152]{2,1,0:T(8,128)(2,1)S(1)}, u32[]{:S(2)}, u32[]{:S(2)}) %collective-permute-start.15) | collective-permute-done | bytes 110624 | tf_op jit(solution)/shard_map/ppermute | solution.py:565
  229.9 4.9 %place_other.3 = f32[2048,768]{1,0:T(8,128)} custom-call(s32[34]{0:T(128)} %pad_add_fusion.s_ref, f32[2048,768]{1,0:T(8,128)} %get-tuple-element.79.whole_ref, f32[1024,768]{1,0:T(8,128)} %collective-permute-done.11.part_ref), custom_call_target="tpu_custom_call", output_to_operand_aliasing={{}: (1, {})} | custom-call | bytes 6291456 | tf_op jit(solution)/shard_map/place_other/pallas_call | solution.py:533
  (127 shorter events, 44.5 us)
Async XLA Ops:
  0.6 22.1 %collective-permute-start.4 = (bf16[768,1536]{1,0:T(8,128)(2,1)}, bf16[768,1536]{1,0:T(8,128)(2,1)S(1)}, u32[]{:S(2)}, u32[]{:S(2)}) collective-permute-start(bf16[768,1536]{1,0:T(8,128)(2,1)} %wuo_hbm.3), channel_id=1, source_target_pairs={{0,1},{1,0},{2,3},{3,2},{4,5},{5,4},{6,7},{7,6},{8,9},{9,8},{10,11... | collective-permute-start | bytes 7077896 | tf_op jit(solution)/shard_map/ppermute | solution.py:568
  1.2 21.6 %collective-permute-start.5 = (bf16[1536,768]{1,0:T(8,128)(2,1)}, bf16[1536,768]{1,0:T(8,128)(2,1)}, u32[]{:S(2)}, u32[]{:S(2)}) collective-permute-start(bf16[1536,768]{1,0:T(8,128)(2,1)} %wdo_hbm.3), channel_id=1, source_target_pairs={{0,1},{1,0},{2,3},{3,2},{4,5},{5,4},{6,7},{7,6},{8,9},{9,8},{10,11... | collective-permute-start | bytes 7077896 | tf_op jit(solution)/shard_map/ppermute | solution.py:568
  1.2 12.6 %collective-permute-start = (bf16[3,768,384]{2,1,0:T(8,128)(2,1)}, bf16[3,768,384]{2,1,0:T(8,128)(2,1)}, u32[]{:S(2)}, u32[]{:S(2)}) collective-permute-start(bf16[3,768,384]{2,1,0:T(8,128)(2,1)} %bitcast.36), channel_id=1, source_target_pairs={{0,1},{1,0},{2,3},{3,2},{4,5},{5,4},{6,7},{7,6},{8,9},{9,8},{10,11... | collective-permute-start | bytes 5308424 | tf_op jit(solution)/shard_map/ppermute | solution.py:568
  1.7 11.0 %collective-permute-start.2 = (f32[1536]{0:T(1024)}, f32[1536]{0:T(1024)S(1)}, u32[]{:S(2)}, u32[]{:S(2)}) collective-permute-start(f32[1536]{0:T(1024)} %param.25), channel_id=1, source_target_pairs={{0,1},{1,0},{2,3},{3,2},{4,5},{5,4},{6,7},{7,6},{8,9},{9,8},{10,11... | collective-permute-start | bytes 18440 | tf_op jit(solution)/shard_map/ppermute | solution.py:568
  1.8 21.0 %collective-permute-start.3 = (bf16[384,768]{1,0:T(8,128)(2,1)}, bf16[384,768]{1,0:T(8,128)(2,1)S(1)}, u32[]{:S(2)}, u32[]{:S(2)}) collective-permute-start(bf16[384,768]{1,0:T(8,128)(2,1)} %woo_hbm.3), channel_id=1, source_target_pairs={{0,1},{1,0},{2,3},{3,2},{4,5},{5,4},{6,7},{7,6},{8,9},{9,8},{10,11... | collective-permute-start | bytes 1769480 | tf_op jit(solution)/shard_map/ppermute | solution.py:568
  99.2 31.1 %collective-permute-start.8 = (bf16[16,48,1536]{2,1,0:T(8,128)(2,1)}, bf16[16,48,1536]{2,1,0:T(8,128)(2,1)S(1)}, u32[]{:S(2)}, u32[]{:S(2)}) collective-permute-start(bf16[16,48,1536]{2,1,0:T(8,128)(2,1)} %get-tuple-element.71), channel_id=1, source_target_pairs={{0,1},{1,0},{2,3},{3,2},{4,5},{5,4},{6,7},{7,6},{8,9},{9,8},{10,11... | collective-permute-start | bytes 7077896 | tf_op jit(solution)/shard_map/ppermute | solution.py:568
  99.4 26.5 %collective-permute-start.25 = (bf16[8,48,1536]{2,1,0:T(8,128)(2,1)}, bf16[8,48,1536]{2,1,0:T(8,128)(2,1)}, u32[]{:S(2)}, u32[]{:S(2)}) collective-permute-start(bf16[8,48,1536]{2,1,0:T(8,128)(2,1)} %get-tuple-element.115), channel_id=1, source_target_pairs={{0,2},{1,5},{2,0},{3,7},{4,6},{5,1},{6,4},{7,3},{8,10},{9,13},{10,... | collective-permute-start | bytes 3538952 | tf_op jit(solution)/shard_map/ppermute | solution.py:565
  102.2 58.7 %collective-permute-start.6 = (f32[1024,768]{1,0:T(8,128)}, f32[1024,768]{1,0:T(8,128)}, u32[]{:S(2)}, u32[]{:S(2)}) collective-permute-start(f32[1024,768]{1,0:T(8,128)} %get-tuple-element.53), channel_id=1, source_target_pairs={{0,1},{1,0},{2,3},{3,2},{4,5},{5,4},{6,7},{7,6},{8,9},{9,8},{10,11... | collective-permute-start | bytes 9437192 | tf_op jit(solution)/shard_map/ppermute | solution.py:568
  103.6 20.2 %collective-permute-start.9 = (bf16[16,48,384]{2,1,0:T(8,128)(2,1)}, bf16[16,48,384]{2,1,0:T(8,128)(2,1)}, u32[]{:S(2)}, u32[]{:S(2)}) collective-permute-start(bf16[16,48,384]{2,1,0:T(8,128)(2,1)} %get-tuple-element.73), channel_id=1, source_target_pairs={{0,1},{1,0},{2,3},{3,2},{4,5},{5,4},{6,7},{7,6},{8,9},{9,8},{10,11... | collective-permute-start | bytes 1769480 | tf_op jit(solution)/shard_map/ppermute | solution.py:568
  128.7 16.5 %collective-permute-start.26 = (bf16[4,48,1536]{2,1,0:T(8,128)(2,1)}, bf16[4,48,1536]{2,1,0:T(8,128)(2,1)}, u32[]{:S(2)}, u32[]{:S(2)}) collective-permute-start(bf16[4,48,1536]{2,1,0:T(8,128)(2,1)} %get-tuple-element.123), channel_id=1, source_target_pairs={{0,4},{1,3},{2,6},{3,1},{4,0},{5,7},{6,2},{7,5},{8,12},{9,11},{10,... | collective-permute-start | bytes 1769480 | tf_op jit(solution)/shard_map/ppermute | solution.py:565
  146.4 9.5 %collective-permute-start.27 = (bf16[2,48,1536]{2,1,0:T(8,128)(2,1)S(1)}, bf16[2,48,1536]{2,1,0:T(8,128)(2,1)S(1)}, u32[]{:S(2)}, u32[]{:S(2)}) collective-permute-start(bf16[2,48,1536]{2,1,0:T(8,128)(2,1)S(1)} %get-tuple-element.129), channel_id=1, source_target_pairs={{0,8},{1,9},{2,10},{3,11},{4,12},{5,13},{6,14},{7,15},{8,0},{9,1},... | collective-permute-start | bytes 884744 | tf_op jit(solution)/shard_map/ppermute | solution.py:565
  149.4 22.2 %collective-permute-start.21 = (bf16[8,48,1920]{2,1,0:T(8,128)(2,1)S(1)}, bf16[8,48,1920]{2,1,0:T(8,128)(2,1)}, u32[]{:S(2)}, u32[]{:S(2)}) collective-permute-start(bf16[8,48,1920]{2,1,0:T(8,128)(2,1)S(1)} %pad_maximum_fusion), channel_id=1, source_target_pairs={{0,2},{1,5},{2,0},{3,7},{4,6},{5,1},{6,4},{7,3},{8,10},{9,13},{10,... | collective-permute-start | bytes 4423688 | tf_op jit(solution)/shard_map/ppermute | solution.py:565
  150.9 23.1 %collective-permute-start.10 = (bf16[16,48,1152]{2,1,0:T(8,128)(2,1)}, bf16[16,48,1152]{2,1,0:T(8,128)(2,1)}, u32[]{:S(2)}, u32[]{:S(2)}) collective-permute-start(bf16[16,48,1152]{2,1,0:T(8,128)(2,1)} %get-tuple-element.75), channel_id=1, source_target_pairs={{0,1},{1,0},{2,3},{3,2},{4,5},{5,4},{6,7},{7,6},{8,9},{9,8},{10,11... | collective-permute-start | bytes 5308424 | tf_op jit(solution)/shard_map/ppermute | solution.py:568
  153.4 5.1 %collective-permute-start.18 = (f32[54,128]{1,0:T(8,128)S(1)}, f32[54,128]{1,0:T(8,128)S(1)}, u32[]{:S(2)}, u32[]{:S(2)}) collective-permute-start(f32[54,128]{1,0:T(8,128)S(1)} %fusion.3), channel_id=1, source_target_pairs={{0,4},{2,6},{4,0},{6,2},{8,12},{10,14},{12,8},{14,10},{16,20},{18,... | collective-permute-start | bytes 82952 | tf_op jit(solution)/shard_map/ppermute | solution.py:658
  155.9 10.8 %collective-permute-start.28 = (bf16[1,48,1536]{2,1,0:T(8,128)(2,1)S(1)}, bf16[1,48,1536]{2,1,0:T(8,128)(2,1)S(1)}, u32[]{:S(2)}, u32[]{:S(2)}) collective-permute-start(bf16[1,48,1536]{2,1,0:T(8,128)(2,1)S(1)} %add_convert_fusion.22), channel_id=1, source_target_pairs={{0,16},{1,17},{2,18},{3,19},{4,20},{5,21},{6,22},{7,23},{8,24},{9,... | collective-permute-start | bytes 442376 | tf_op jit(solution)/shard_map/ppermute | solution.py:565
  159.3 6.6 %collective-permute-start.19 = (f32[54,128]{1,0:T(8,128)S(1)}, f32[54,128]{1,0:T(8,128)S(1)}, u32[]{:S(2)}, u32[]{:S(2)}) collective-permute-start(f32[54,128]{1,0:T(8,128)S(1)} %fusion.4), channel_id=1, source_target_pairs={{0,8},{2,10},{4,12},{6,14},{8,0},{10,2},{12,4},{14,6},{16,24},{18,... | collective-permute-start | bytes 82952 | tf_op jit(solution)/shard_map/ppermute | solution.py:658
  173.4 23.8 %collective-permute-start.22 = (bf16[4,48,1920]{2,1,0:T(8,128)(2,1)S(1)}, bf16[4,48,1920]{2,1,0:T(8,128)(2,1)}, u32[]{:S(2)}, u32[]{:S(2)}) collective-permute-start(bf16[4,48,1920]{2,1,0:T(8,128)(2,1)S(1)} %get-tuple-element.121), channel_id=1, source_target_pairs={{0,4},{1,3},{2,6},{3,1},{4,0},{5,7},{6,2},{7,5},{8,12},{9,11},{10,... | collective-permute-start | bytes 2211848 | tf_op jit(solution)/shard_map/ppermute | solution.py:565
  176.8 23.3 %collective-permute-start.12 = (bf16[8,48,1152]{2,1,0:T(8,128)(2,1)}, bf16[8,48,1152]{2,1,0:T(8,128)(2,1)S(1)}, u32[]{:S(2)}, u32[]{:S(2)}) collective-permute-start(bf16[8,48,1152]{2,1,0:T(8,128)(2,1)} %get-tuple-element.119), channel_id=1, source_target_pairs={{0,2},{1,5},{2,0},{3,7},{4,6},{5,1},{6,4},{7,3},{8,10},{9,13},{10,... | collective-permute-start | bytes 2654216 | tf_op jit(solution)/shard_map/ppermute | solution.py:565
  189.9 40.0 %collective-permute-start.11 = (f32[1024,768]{1,0:T(8,128)}, f32[1024,768]{1,0:T(8,128)}, u32[]{:S(2)}, u32[]{:S(2)}) collective-permute-start(f32[1024,768]{1,0:T(8,128)} %get-tuple-element.80), channel_id=1, source_target_pairs={{0,1},{1,0},{2,3},{3,2},{4,5},{5,4},{6,7},{7,6},{8,9},{9,8},{10,11... | collective-permute-start | bytes 9437192 | tf_op jit(solution)/shard_map/ppermute | solution.py:568
  198.5 11.3 %collective-permute-start.23 = (bf16[2,48,1920]{2,1,0:T(8,128)(2,1)S(1)}, bf16[2,48,1920]{2,1,0:T(8,128)(2,1)S(1)}, u32[]{:S(2)}, u32[]{:S(2)}) collective-permute-start(bf16[2,48,1920]{2,1,0:T(8,128)(2,1)S(1)} %get-tuple-element.127), channel_id=1, source_target_pairs={{0,8},{1,9},{2,10},{3,11},{4,12},{5,13},{6,14},{7,15},{8,0},{9,1},... | collective-permute-start | bytes 1105928 | tf_op jit(solution)/shard_map/ppermute | solution.py:565
  200.3 11.4 %collective-permute-start.13 = (bf16[4,48,1152]{2,1,0:T(8,128)(2,1)S(1)}, bf16[4,48,1152]{2,1,0:T(8,128)(2,1)S(1)}, u32[]{:S(2)}, u32[]{:S(2)}) collective-permute-start(bf16[4,48,1152]{2,1,0:T(8,128)(2,1)S(1)} %get-tuple-element.125), channel_id=1, source_target_pairs={{0,4},{1,3},{2,6},{3,1},{4,0},{5,7},{6,2},{7,5},{8,12},{9,11},{10,... | collective-permute-start | bytes 1327112 | tf_op jit(solution)/shard_map/ppermute | solution.py:565
  209.8 11.2 %collective-permute-start.24 = (bf16[1,48,1920]{2,1,0:T(8,128)(2,1)S(1)}, bf16[1,48,1920]{2,1,0:T(8,128)(2,1)S(1)}, u32[]{:S(2)}, u32[]{:S(2)}) collective-permute-start(bf16[1,48,1920]{2,1,0:T(8,128)(2,1)S(1)} %add_convert_fusion.20), channel_id=1, source_target_pairs={{0,16},{1,17},{2,18},{3,19},{4,20},{5,21},{6,22},{7,23},{8,24},{9,... | collective-permute-start | bytes 552968 | tf_op jit(solution)/shard_map/ppermute | solution.py:565
  211.9 10.2 %collective-permute-start.14 = (bf16[2,48,1152]{2,1,0:T(8,128)(2,1)S(1)}, bf16[2,48,1152]{2,1,0:T(8,128)(2,1)S(1)}, u32[]{:S(2)}, u32[]{:S(2)}) collective-permute-start(bf16[2,48,1152]{2,1,0:T(8,128)(2,1)S(1)} %get-tuple-element.133), channel_id=1, source_target_pairs={{0,8},{1,9},{2,10},{3,11},{4,12},{5,13},{6,14},{7,15},{8,0},{9,1},... | collective-permute-start | bytes 663560 | tf_op jit(solution)/shard_map/ppermute | solution.py:565
  222.1 6.9 %collective-permute-start.15 = (bf16[1,48,1152]{2,1,0:T(8,128)(2,1)S(1)}, bf16[1,48,1152]{2,1,0:T(8,128)(2,1)S(1)}, u32[]{:S(2)}, u32[]{:S(2)}) collective-permute-start(bf16[1,48,1152]{2,1,0:T(8,128)(2,1)S(1)} %add_convert_fusion.24), channel_id=1, source_target_pairs={{0,16},{1,17},{2,18},{3,19},{4,20},{5,21},{6,22},{7,23},{8,24},{9,... | collective-permute-start | bytes 331784 | tf_op jit(solution)/shard_map/ppermute | solution.py:565
  (23 other events, 185.2 us)

commit v2 on v0

v2 whole, which is shorter than its diff:
```python
import functools

import jax
import jax.numpy as jnp
from jax import lax
from jax.experimental import pallas as pl
from jax.experimental.pallas import tpu as pltpu
from jax.sharding import PartitionSpec as P

HEAD_DIM = 64
SEG = 128
EPS = 1e-05
LANES = 128
F32 = jnp.float32
LOW = jnp.bfloat16
OWN = jnp.bfloat16
FF_CHUNK = 768
BLOCK = 256
VMEM_LIMIT = 60 * 1024 * 1024


def mm(first, second):
    return jnp.dot(first, second, preferred_element_type=F32)


def mm_nt(first, second):
    return lax.dot_general(first, second, (((1,), (1,)), ((), ())), preferred_element_type=F32)


def mm_tn(first, second):
    return lax.dot_general(first, second, (((0,), (0,)), ((), ())), preferred_element_type=F32)


def fold_rows(values):
    rows, width = values.shape
    return jnp.sum(values.reshape(rows // 8, 8, width), 0)


def gelu_pair(pre):
    below = 0.5 + 0.5 * lax.erf(pre * 0.7071067811865476)
    bell = jnp.exp2(pre * pre * (-0.5 * 1.4426950408889634))
    return pre * below, below + pre * bell * 0.3989422804014327


def const_spec(shape):
    zeros = (0,) * len(shape)
    return pl.BlockSpec(shape, lambda i, s: zeros, pipeline_mode=pl.Buffered(1))


def row_spec(block, width):
    return pl.BlockSpec((block, width), lambda i, s: (i, 0))


def cost(micros):
    return pl.CostEstimate(flops=0, bytes_accessed=int(micros * 3.69e6), transcendentals=0)


def params():
    return pltpu.CompilerParams(dimension_semantics=("arbitrary",), vmem_limit_bytes=VMEM_LIMIT)


def slots_of(width, parts):
    share = width // parts
    return (parts, share) if share % 16 == 0 else (1, width)


def arrange(grad, table, parts):
    if grad.shape[0] == parts:
        return grad
    spots = jnp.zeros((parts,), jnp.int32).at[table].set(jnp.arange(parts, dtype=jnp.int32))
    return jnp.take(grad.reshape(parts, -1, grad.shape[2]), spots, axis=0)


class Fetch:
    def __init__(self, sources, targets, sems):
        self.copies = [pltpu.make_async_copy(s, t, sems.at[i]) for i, (s, t) in enumerate(zip(sources, targets))]

    def start(self):
        @pl.when(pl.program_id(0) == 0)
        def _():
            for copy in self.copies:
                copy.start()

    def wait(self, *which):
        @pl.when(pl.program_id(0) == 0)
        def _():
            for i in which:
                self.copies[i].wait()


def fixed(shape):
    return pl.BlockSpec(shape, lambda i, s: (0,) * len(shape))


def spread(grad, out_ref, lanes, table, parts):
    if out_ref.shape[0] == 1:
        out_ref[0, :, lanes] = grad
        return
    share = grad.shape[0] // parts
    for part in range(parts):
        out_ref[table(part), :, lanes] = grad[part * share : (part + 1) * share]


def table_of(s_ref, kind, side, parts):
    return lambda part: s_ref[2 + (2 * kind + side) * parts + part]


def split_heads(values, masks):
    return jnp.concatenate([values * masks[0], values * masks[1]], 0)


def head_masks():
    left = lax.broadcasted_iota(jnp.int32, (SEG, LANES), 1) < HEAD_DIM
    return jnp.where(left, 1.0, 0.0).astype(LOW), jnp.where(left, 0.0, 1.0).astype(LOW)


ALL = slice(None)
ANY = pl.BlockSpec(memory_space=pl.ANY)


def row_of(ref):
    return ref[...].reshape(1, ref.shape[0])


def attn_fwd_kernel(block, rows, s_ref, x_ref, bo_ref, bt_ref, wo_hbm, wt_hbm, qkv_ref, p_ref, a_ref, w_ref, sems):
    cols = wo_hbm.shape[2]
    width = 2 * cols
    step = pl.program_id(0)
    fetch = Fetch(
        [w.at[kind] for kind in range(3) for w in (wo_hbm, wt_hbm)],
        [w_ref.at[:, (2 * kind + side) * cols : (2 * kind + side + 1) * cols] for kind in range(3) for side in range(2)],
        sems,
    )
    fetch.start()
    fetch.wait(*range(6))
    linear = mm(x_ref[...], w_ref[...])
    bias_q, bias_v = (jnp.concatenate([bo_ref[i : i + 1, :], bt_ref[i : i + 1, :]], 1) for i in range(2))
    q = ((linear[:, :width] + bias_q) * (HEAD_DIM**-0.5)).astype(LOW)
    k = linear[:, width : 2 * width].astype(LOW)
    v = (linear[:, 2 * width :] + bias_v).astype(LOW)
    qkv_ref[:, :width] = q
    qkv_ref[:, width : 2 * width] = k
    qkv_ref[:, 2 * width :] = v
    masks = head_masks()
    first_slot = s_ref[0] * rows + step * block
    for seg in range(block // SEG):
        at = slice(seg * SEG, (seg + 1) * SEG)
        slots = lax.broadcasted_iota(jnp.int32, (SEG, 2 * SEG), 0) + (first_slot + seg * SEG)
        bias = jnp.where(slots < s_ref[1], 0.0, -30000.0)
        for pair in range(width // LANES):
            lanes = slice(pair * LANES, (pair + 1) * LANES)
            scores = mm_nt(k[at, lanes], split_heads(q[at, lanes], masks)) + bias
            grown = jnp.exp(scores - jnp.max(scores, 0, keepdims=True))
            probs = (grown * (1.0 / jnp.sum(grown, 0, keepdims=True))).astype(LOW)
            p_ref[at, 2 * pair * SEG : 2 * (pair + 1) * SEG] = probs
            stacked = jnp.concatenate([probs[:, :SEG], probs[:, SEG:]], 0)
            a_ref[at, lanes] = mm_tn(stacked, split_heads(v[at, lanes], masks)).astype(LOW)


def attn_fwd(scal, tokens, w, b, rows, block):
    cols = w[0].shape[2]
    width = tokens.shape[1]
    steps = rows // block
    outs = [6 * cols, 2 * cols // HEAD_DIM * SEG, 2 * cols]
    return pl.pallas_call(
        functools.partial(attn_fwd_kernel, block, rows),
        grid_spec=pltpu.PrefetchScalarGridSpec(
            num_scalar_prefetch=1,
            grid=(steps,),
            in_specs=[pl.BlockSpec((block, width), lambda i, s: (s[0] * steps + i, 0))]
            + [const_spec(b[0].shape)] * 2
            + [ANY, ANY],
            out_specs=[row_spec(block, w) for w in outs],
            scratch_shapes=[pltpu.VMEM((width, 6 * cols), LOW), pltpu.SemaphoreType.DMA((6,))],
        ),
        out_shape=[jax.ShapeDtypeStruct((rows, w), LOW) for w in outs],
        compiler_params=params(),
        cost_estimate=cost(14),
        name="attn_fwd",
    )(scal, tokens, *b, *w)


def ffn_spots(half, chunk):
    return [
        (slice(side * half + start, side * half + start + chunk), side, slice(start, start + chunk))
        for side in range(2)
        for start in range(0, half, chunk)
    ]


def ffn_fwd_kernel(
    block, rows, chunk, parts, steps,
    s_ref, x_ref, g_ref, att_ref, bo_ref, bt_ref, bout_ref, g1_ref, h1_ref, bdown_ref, g2_ref, h2_ref,
    woo_hbm, wot_hbm, wuo_hbm, wut_hbm, wdo_hbm, wdt_hbm,
    out_ref, own_ref, gp_ref, low_ref, hat_ref, rs_ref, dmlp_ref, sums_ref, dt_ref, do_ref,
    wo_ref, wu_ref, wd_ref, sems, hid_ref, all_ref,
):
    step = pl.program_id(0)
    half = wuo_hbm.shape[1]
    cols = woo_hbm.shape[0]
    spots = ffn_spots(half, chunk)
    sources, targets = [woo_hbm, wot_hbm], [wo_ref.at[:cols], wo_ref.at[cols:]]
    for spot, side, local in spots:
        sources += [(wuo_hbm, wut_hbm)[side].at[:, local], (wdo_hbm, wdt_hbm)[side].at[local]]
        targets += [wu_ref.at[:, spot], wd_ref.at[spot]]
    fetch = Fetch(sources, targets, sems)
    fetch.start()

    @pl.when(step == 0)
    def _():
        sums_ref[...] = jnp.zeros_like(sums_ref)

    @pl.when(step < steps)
    def _():
        fetch.wait(0, 1)
        mine = pl.ds(pl.multiple_of(step * block, block), block)
        h1 = x_ref[...].astype(F32) + mm(att_ref[...], wo_ref[...]) + row_of(bout_ref)
        center = h1 - jnp.mean(h1, -1, keepdims=True)
        scale = lax.rsqrt(jnp.mean(center * center, -1, keepdims=True) + EPS)
        hat = center * scale
        hat_ref[...] = hat.astype(LOW)
        rs_ref[...] = jnp.broadcast_to(scale, rs_ref.shape)
        normed = hat * row_of(g1_ref) + row_of(h1_ref)
        low = normed.astype(LOW)
        low_ref[...] = low
        total = normed + row_of(bdown_ref)
        for i, (spot, side, local) in enumerate(spots):
            fetch.wait(2 + 2 * i, 3 + 2 * i)
            bias = (bo_ref, bt_ref)[side][pl.ds(local.start, chunk)].reshape(1, chunk)
            hidden, slope = gelu_pair(mm(low, wu_ref[:, spot]) + bias)
            hidden = hidden.astype(LOW)
            hid_ref[mine, spot] = hidden
            gp_ref[:, spot] = slope.astype(LOW)
            total = total + mm(hidden, wd_ref[spot, :])
        center = total - jnp.mean(total, -1, keepdims=True)
        scale = lax.rsqrt(jnp.mean(center * center, -1, keepdims=True) + EPS)
        hat = center * scale
        gain_two = row_of(g2_ref)
        result = (hat * gain_two + row_of(h2_ref)).astype(OWN)
        out_ref[...] = result.astype(F32)
        own_ref[...] = result
        slots = lax.broadcasted_iota(jnp.int32, (block, 1), 0) + (s_ref[0] * rows + step * block)
        cot = jnp.where(slots < s_ref[1], g_ref[...], 0.0)
        inner = cot * gain_two
        d_h2 = scale * (
            inner - jnp.mean(inner, -1, keepdims=True) - hat * jnp.mean(inner * hat, -1, keepdims=True)
        )
        d_mlp = d_h2.astype(LOW)
        dmlp_ref[...] = d_mlp
        all_ref[mine, :] = d_mlp
        sums_ref[0:8, :] += fold_rows(cot * hat)
        sums_ref[8:16, :] += fold_rows(cot)
        sums_ref[16:24, :] += fold_rows(d_h2)

    wide = dt_ref.shape[2]
    at = steps
    for side in (1, 0):
        for start in range(side * half, (side + 1) * half, wide):

            @pl.when(step == at)
            def _():
                grad = mm_tn(all_ref[...], hid_ref[:, start : start + wide]).astype(LOW)
                spread(grad, (do_ref, dt_ref)[side], ALL, table_of(s_ref, 0, side, parts), parts)

            at += 1


def ffn_fwd(scal, tokens, grad_out, att, w_out, w_up, b_up, w_down, vec, rows, block, chunk, wide, parts):
    width = tokens.shape[1]
    steps = rows // block
    half = w_up[0].shape[1]
    pieces = half // wide
    row = lambda i: jnp.minimum(i, steps - 1)
    mine = lambda i, s: (s[0] * steps + row(i), 0)
    rows_of = lambda w: pl.BlockSpec((block, w), lambda i, s: (row(i), 0))
    lead = slots_of(width, parts)
    weights = [*w_out, *w_up, *w_down]
    small = [*b_up, *vec]
    outs = [(width, OWN), (2 * half, LOW), (width, LOW), (width, LOW), (LANES, F32), (width, LOW)]
    piece_at = lambda k: pl.BlockSpec((*lead, wide), lambda i, s: (0, 0, jnp.clip(i - steps - k * pieces, 0, pieces - 1)))
    return pl.pallas_call(
        functools.partial(ffn_fwd_kernel, block, rows, chunk, parts, steps),
        grid_spec=pltpu.PrefetchScalarGridSpec(
            num_scalar_prefetch=1,
            grid=(steps + 2 * pieces,),
            in_specs=[pl.BlockSpec((block, width), mine), pl.BlockSpec((block, width), mine), rows_of(att.shape[1])]
            + [const_spec(v.shape) for v in small]
            + [ANY] * 6,
            out_specs=[pl.BlockSpec((block, width), mine)]
            + [rows_of(w) for w, _ in outs]
            + [fixed((24, width)), piece_at(0), piece_at(1)],
            scratch_shapes=[
                pltpu.VMEM((att.shape[1], width), LOW),
                pltpu.VMEM((width, 2 * half), LOW),
                pltpu.VMEM((2 * half, width), LOW),
                pltpu.SemaphoreType.DMA((2 + 4 * half // chunk,)),
                pltpu.VMEM((rows, 2 * half), LOW),
                pltpu.VMEM((rows, width), LOW),
            ],
        ),
        out_shape=[jax.ShapeDtypeStruct((2 * rows, width), F32)]
        + [jax.ShapeDtypeStruct((rows, w), t) for w, t in outs]
        + [jax.ShapeDtypeStruct((24, width), F32)]
        + [jax.ShapeDtypeStruct((*lead, half), LOW)] * 2,
        compiler_params=params(),
        cost_estimate=cost(35),
        name="ffn_fwd",
    )(scal, tokens, grad_out, att, *small, *weights)


def ffn_bwd_kernel(
    block, chunk, parts, steps,
    s_ref, dmlp_ref, gp_ref, hat_ref, rs_ref, g1_ref, woo_hbm, wot_hbm, wuo_hbm, wut_hbm, wdo_hbm, wdt_hbm, low_hbm, att_hbm,
    dh1_ref, datt_ref, sums_ref, bup_ref, ut_ref, uo_ref, ot_ref, oo_ref,
    wo_ref, wu_ref, wd_ref, low_ref, att_ref, sems, dpre_ref, dbr_ref,
):
    step = pl.program_id(0)
    half = wuo_hbm.shape[1]
    cols = woo_hbm.shape[0]
    spots = ffn_spots(half, chunk)
    sources, targets = [], []
    for spot, side, local in spots:
        sources += [(wdo_hbm, wdt_hbm)[side].at[local], (wuo_hbm, wut_hbm)[side].at[:, local]]
        targets += [wd_ref.at[spot], wu_ref.at[:, spot]]
    tail = len(sources)
    sources += [woo_hbm, wot_hbm, low_hbm, att_hbm]
    targets += [wo_ref.at[:cols], wo_ref.at[cols:], low_ref, att_ref]
    fetch = Fetch(sources, targets, sems)
    fetch.start()

    @pl.when(step == 0)
    def _():
        sums_ref[...] = jnp.zeros_like(sums_ref)
        bup_ref[...] = jnp.zeros_like(bup_ref)

    @pl.when(step < steps)
    def _():
        mine = pl.ds(pl.multiple_of(step * block, block), block)
        d_mlp = dmlp_ref[...]
        total = d_mlp.astype(F32)
        for i, (spot, side, local) in enumerate(spots):
            fetch.wait(2 * i, 2 * i + 1)
            d_pre = (mm_nt(d_mlp, wd_ref[spot, :]) * gp_ref[:, spot].astype(F32)).astype(LOW)
            dpre_ref[mine, spot] = d_pre
            bup_ref[:, spot] += fold_rows(d_pre.astype(F32))
            total = total + mm_nt(d_pre, wu_ref[:, spot])
        hat = hat_ref[...].astype(F32)
        inner = total * row_of(g1_ref)
        d_h1 = rs_ref[:, 0:1] * (
            inner - jnp.mean(inner, -1, keepdims=True) - hat * jnp.mean(inner * hat, -1, keepdims=True)
        )
        sums_ref[0:8, :] += fold_rows(total * hat)
        sums_ref[8:16, :] += fold_rows(total)
        sums_ref[16:24, :] += fold_rows(d_h1)
        dh1_ref[...] = d_h1
        low = d_h1.astype(LOW)
        dbr_ref[mine, :] = low
        fetch.wait(tail, tail + 1)
        datt_ref[...] = mm_nt(low, wo_ref[...]).astype(LOW)

    @pl.when(step == steps - 1)
    def _():
        for i in (tail + 2, tail + 3):
            fetch.copies[i].wait()

    wide = ut_ref.shape[2]
    at = steps
    for side in (1, 0):
        for start in range(side * half, (side + 1) * half, wide):

            @pl.when(step == at)
            def _():
                grad = mm_tn(low_ref[...], dpre_ref[:, start : start + wide]).astype(LOW)
                spread(grad, (uo_ref, ut_ref)[side], ALL, table_of(s_ref, 1, side, parts), parts)

            at += 1

    @pl.when(step == at)
    def _():
        grad = mm_tn(dbr_ref[...], att_ref[...]).astype(LOW)
        spread(grad[:, :cols], oo_ref, ALL, table_of(s_ref, 1, 0, parts), parts)
        spread(grad[:, cols:], ot_ref, ALL, table_of(s_ref, 1, 1, parts), parts)


def ffn_bwd(scal, d_mlp, slope, hat, scale, normed_low, att, w_out, w_up, w_down, gain_one, block, chunk, wide, parts):
    rows, width = d_mlp.shape
    steps = rows // block
    half = w_up[0].shape[1]
    pieces = half // wide
    cols = w_out[0].shape[0]
    rows_of = lambda w: pl.BlockSpec((block, w), lambda i, s: (jnp.minimum(i, steps - 1), 0))
    moving = [d_mlp, slope, hat, scale]
    lead = slots_of(width, parts)
    piece_at = lambda k: pl.BlockSpec((*lead, wide), lambda i, s: (0, 0, jnp.clip(i - steps - k * pieces, 0, pieces - 1)))
    return pl.pallas_call(
        functools.partial(ffn_bwd_kernel, block, chunk, parts, steps),
        grid_spec=pltpu.PrefetchScalarGridSpec(
            num_scalar_prefetch=1,
            grid=(steps + 2 * pieces + 1,),
            in_specs=[rows_of(m.shape[1]) for m in moving] + [const_spec(gain_one.shape)] + [ANY] * 8,
            out_specs=[rows_of(width), rows_of(2 * cols), fixed((24, width)), fixed((8, 2 * half))]
            + [piece_at(0), piece_at(1)]
            + [fixed((*lead, cols))] * 2,
            scratch_shapes=[
                pltpu.VMEM((2 * cols, width), LOW),
                pltpu.VMEM((width, 2 * half), LOW),
                pltpu.VMEM((2 * half, width), LOW),
                pltpu.VMEM((rows, width), LOW),
                pltpu.VMEM((rows, 2 * cols), LOW),
                pltpu.SemaphoreType.DMA((4 + 4 * half // chunk,)),
                pltpu.VMEM((rows, 2 * half), LOW),
                pltpu.VMEM((rows, width), LOW),
            ],
        ),
        out_shape=[
            jax.ShapeDtypeStruct((rows, width), F32),
            jax.ShapeDtypeStruct((rows, 2 * cols), LOW),
            jax.ShapeDtypeStruct((24, width), F32),
            jax.ShapeDtypeStruct((8, 2 * half), F32),
        ]
        + [jax.ShapeDtypeStruct((*lead, half), LOW)] * 2
        + [jax.ShapeDtypeStruct((*lead, cols), LOW)] * 2,
        compiler_params=params(),
        cost_estimate=cost(32),
        name="ffn_bwd",
    )(scal, *moving, gain_one, *w_out, *w_up, *w_down, normed_low, att)


def attn_bwd_kernel(block, side, parts, steps, s_ref, *refs):
    q_ref, k_ref, v_ref, p_ref, da_ref, base_ref, x_hbm, w_hbm = refs[:8]
    if side:
        part_ref, _, sum_ref, grad_ref, tok_ref, whole_ref = refs[8:-5]
    else:
        two_ref, one_ref, bup_ref, other_ref, sum_ref, grad_ref, tok_ref, own_ref, keep_ref, send_ref = refs[8:-5]
    x_ref, w_ref, sems, all_ref, dl_ref = refs[-5:]
    step = pl.program_id(0)
    cols = da_ref.shape[1]
    rows = x_ref.shape[0]
    fetch = Fetch(
        [w_hbm.at[kind] for kind in range(3)] + [x_hbm.at[pl.ds(pl.multiple_of(s_ref[0] * rows, rows), rows)]],
        [w_ref.at[:, kind * cols : (kind + 1) * cols] for kind in range(3)] + [x_ref],
        sems,
    )
    fetch.start()

    @pl.when(step == 0)
    def _():
        sum_ref[...] = jnp.zeros_like(sum_ref)

    @pl.when(step < steps)
    def _():
        if side:
            whole_ref[...] = part_ref[...].astype(whole_ref.dtype)
        masks = head_masks()
        for seg in range(block // SEG):
            at = slice(seg * SEG, (seg + 1) * SEG)
            for pair in range(cols // LANES):
                lanes = slice(pair * LANES, (pair + 1) * LANES)
                k_lanes = slice(cols + pair * LANES, cols + (pair + 1) * LANES)
                v_lanes = slice(2 * cols + pair * LANES, 2 * cols + (pair + 1) * LANES)
                low_probs = p_ref[at, 2 * pair * SEG : 2 * (pair + 1) * SEG]
                probs = low_probs.astype(F32)
                d_att = split_heads(da_ref[at, lanes], masks)
                d_probs = mm_nt(v_ref[at, lanes], d_att)
                d_scores = (probs * (d_probs - jnp.sum(probs * d_probs, 0, keepdims=True))).astype(LOW)
                d_v = mm(low_probs, d_att).astype(LOW)
                d_k = mm(d_scores, split_heads(q_ref[at, lanes], masks)).astype(LOW)
                stacked = jnp.concatenate([d_scores[:, :SEG], d_scores[:, SEG:]], 0)
                d_q = (mm_tn(stacked, split_heads(k_ref[at, lanes], masks)) * (HEAD_DIM**-0.5)).astype(LOW)
                dl_ref[at, lanes] = d_q
                dl_ref[at, k_lanes] = d_k
                dl_ref[at, v_lanes] = d_v
                sum_ref[:, lanes] += fold_rows(d_q.astype(F32))
                sum_ref[:, k_lanes] += fold_rows(d_v.astype(F32))
        all_ref[pl.ds(pl.multiple_of(step * block, block), block), :] = dl_ref[...]
        fetch.wait(0, 1, 2)
        total = base_ref[...] + mm_nt(dl_ref[...], w_ref[...])
        if side:
            tok_ref[...] = total
        else:
            total = total.astype(OWN)
            tok_ref[...] = total.astype(F32)
            own_ref[...] = total

    @pl.when(step == steps)
    def _():
        fetch.copies[3].wait()
        grad = mm_tn(x_ref[...], all_ref[...]).astype(LOW)
        spread(grad, grad_ref, ALL, table_of(s_ref, 0, side, parts), parts)
        if not side:
            half = bup_ref.shape[1] // 2
            width = one_ref.shape[1]
            for to, ref, sum_of in ((0, keep_ref, sum_ref), (1, send_ref, other_ref)):
                ref[...] = jnp.zeros_like(ref)
                at = 0
                pieces = [(norm, 8 * group, 0, width) for norm in (two_ref, one_ref) for group in range(3)]
                pieces += [(bup_ref, 0, to * half, half), (sum_of, 0, 0, 2 * cols)]
                for source, top, start, count in pieces:
                    total = jnp.sum(source[top : top + 8, start : start + count], 0, keepdims=True)
                    for piece in range(count // LANES):
                        ref[at : at + 1, :] = total[:, piece * LANES : (piece + 1) * LANES]
                        at += 1


def attn_bwd(scal, qkv, probs, d_att, base, w, extra, tokens, side, block, parts):
    rows = qkv.shape[0]
    width = tokens.shape[1]
    cols = d_att.shape[1] // 2
    steps = rows // block
    row = lambda i: jnp.minimum(i, steps - 1)
    part_of = lambda w, at: pl.BlockSpec((block, w), lambda i, s: (row(i), at))
    lead = slots_of(width, parts)
    in_specs = [part_of(cols, 2 * kind + side) for kind in range(3)] + [part_of(probs.shape[1] // 2, side), part_of(cols, side)]
    in_specs += [part_of(width, 0), ANY, ANY]
    out_specs = [fixed((8, 2 * cols)), fixed((*lead, 3 * cols))]
    out_shape = [jax.ShapeDtypeStruct((8, 2 * cols), F32), jax.ShapeDtypeStruct((*lead, 3 * cols), LOW)]
    if side:
        in_specs += [part_of(width, 0), ANY]
        out_specs += [part_of(width, 0), pl.BlockSpec((block, width), lambda i, s: ((1 - s[0]) * steps + row(i), 0))]
        out_shape += [jax.ShapeDtypeStruct((rows, width), F32), jax.ShapeDtypeStruct(extra[1].shape, F32)]
    else:
        in_specs += [const_spec(m.shape) for m in extra]
        small = -(-(6 * width + extra[2].shape[1] // 2 + 2 * cols) // (8 * LANES)) * 8
        out_specs += [pl.BlockSpec((block, width), lambda i, s: (s[0] * steps + row(i), 0)), part_of(width, 0)]
        out_specs += [fixed((small, LANES))] * 2
        out_shape += [jax.ShapeDtypeStruct((2 * rows, width), F32), jax.ShapeDtypeStruct((rows, width), OWN)]
        out_shape += [jax.ShapeDtypeStruct((small, LANES), F32)] * 2
    return pl.pallas_call(
        functools.partial(attn_bwd_kernel, block, side, parts, steps),
        grid_spec=pltpu.PrefetchScalarGridSpec(
            num_scalar_prefetch=1,
            grid=(steps + 1,),
            in_specs=in_specs,
            out_specs=out_specs,
            scratch_shapes=[
                pltpu.VMEM((rows, width), LOW),
                pltpu.VMEM((width, 3 * cols), LOW),
                pltpu.SemaphoreType.DMA((4,)),
                pltpu.VMEM((rows, 3 * cols), LOW),
                pltpu.VMEM((block, 3 * cols), LOW),
            ],
        ),
        out_shape=out_shape,
        input_output_aliases={10: 3} if side else {},
        compiler_params=params(),
        cost_estimate=cost(15),
        name="attn_bwd",
    )(scal, qkv, qkv, qkv, probs, d_att, base, tokens, w, *extra)


def place_kernel(s_ref, whole_ref, part_ref, out_ref):
    out_ref[...] = part_ref[...].astype(out_ref.dtype)


def place_other(scal, whole, piece, block):
    rows, width = piece.shape
    steps = rows // block
    return pl.pallas_call(
        place_kernel,
        grid_spec=pltpu.PrefetchScalarGridSpec(
            num_scalar_prefetch=1,
            grid=(steps,),
            in_specs=[ANY, row_spec(block, width)],
            out_specs=pl.BlockSpec((block, width), lambda i, s: ((1 - s[0]) * steps + i, 0)),
        ),
        out_shape=jax.ShapeDtypeStruct(whole.shape, F32),
        input_output_aliases={1: 0},
        compiler_params=params(),
        cost_estimate=cost(4),
        name="place_other",
    )(scal, whole, piece)


def shards(
    n_docs, tokens, grad_out, live_tokens, w_qkv, b_qv, w_out, b_out, gain_one, shift_one, w_up, b_up, w_down, b_down,
    gain_two, shift_two,
):
    c = lax.axis_index("heads")
    me = lax.axis_index("docs")
    rows = tokens.shape[0] // 2
    bits = n_docs.bit_length() - 1
    rest = list(range(2, bits))
    orders = [[[0, 1, *rest], [1, 0, *rest]]] * 2

    def step(value, kind, stage):
        pairs = [(d * 2 + h, (d ^ (1 << orders[kind][h][stage])) * 2 + h) for d in range(n_docs) for h in range(2)]
        return lax.ppermute(value, ("docs", "heads"), pairs)

    def swap(value):
        return lax.ppermute(value, "heads", [(0, 1), (1, 0)])

    def after(value, *before):
        return lax.optimization_barrier((value, *before))[0]

    def table_for(kind, core):
        away = jnp.arange(n_docs, dtype=jnp.int32) ^ me
        slots = []
        for order in orders[kind]:
            slot = jnp.zeros((n_docs,), jnp.int32)
            for place, bit in enumerate(order):
                slot = slot | (((away >> bit) & 1) << (bits - 1 - place))
            slots.append(slot)
        return jnp.where(core == 0, slots[0], slots[1])

    tables = [table_for(kind, core) for kind in range(2) for core in (c, 1 - c)]
    scal = jnp.concatenate([c[None].astype(jnp.int32), live_tokens, *tables])

    w_qkv = jnp.transpose(w_qkv, (1, 0, 2))
    w_qkv2 = (w_qkv, swap(w_qkv))
    b_qv2 = (b_qv, swap(b_qv))
    b_up2 = (b_up, swap(b_up))
    w_out, w_up, w_down = after((w_out, w_up, w_down), w_qkv2[1], b_qv2[1], b_up2[1])
    w_out2 = (w_out, swap(w_out))
    w_up2 = (w_up, swap(w_up))
    w_down2 = (w_down, swap(w_down))
    vec = (b_out, gain_one, shift_one, b_down, gain_two, shift_two)

    def add(left, right):
        return (left.astype(F32) + right.astype(F32)).astype(LOW)

    def first_sum(kind, pairs):
        half = n_docs // 2
        parts = [(arrange(own, tables[2 * kind], n_docs), arrange(swap(other), tables[2 * kind], n_docs)) for own, other in pairs]
        cut = lambda at: jnp.concatenate([add(own[at], other[at]) for own, other in parts], 2)
        return cut(slice(half, None)), cut(slice(None, half))

    def next_sum(keep, came):
        half = keep.shape[0] // 2
        if not half:
            return (keep.astype(F32) + came.astype(F32))[0]
        return add(keep[half:], came[half:]), add(keep[:half], came[:half])

    half = w_up.shape[1]
    cols = w_out.shape[0]
    qkv, probs, att = attn_fwd(scal, tokens, w_qkv2, b_qv2, rows, BLOCK)
    def stage_of(kind, pair, stage, *before):
        return next_sum(after(pair[1], *before), step(pair[0], kind, stage))

    layer_out, layer_own, slope, normed_low, hat, scale, d_mlp, sums_two, down_other, down_own = ffn_fwd(
        scal, tokens, grad_out, att, w_out2, w_up2, b_up2, w_down2, vec, rows, BLOCK, FF_CHUNK, 768, n_docs
    )
    down = first_sum(0, [(down_own, down_other)])
    d_mlp = after(d_mlp, down[0])
    d_h1, d_att, sums_one, sums_up, up_other, up_own, out_other, out_own = ffn_bwd(
        scal, d_mlp, slope, hat, scale, normed_low, att, w_out2, w_up2, w_down2, gain_one, BLOCK, FF_CHUNK, 768, n_docs
    )
    down = stage_of(0, down, 0, up_own)
    up_own, up_other, out_own, out_other, layer_own = after((up_own, up_other, out_own, out_other, layer_own), down[0])
    up = first_sum(1, [(up_own, up_other), (out_own, out_other)])
    sums_other, qkv_other, d_tokens, layer_out = attn_bwd(
        scal, qkv, probs, after(d_att, *up), d_h1, w_qkv2[1], (swap(layer_own), layer_out), tokens, 1, BLOCK, n_docs
    )
    down = stage_of(0, down, 1, qkv_other)
    qkv_other, keep_up = after((qkv_other, up[1]), down[0])
    up = stage_of(1, (up[0], keep_up), 0)
    sums = (sums_two, sums_one, sums_up, sums_other)
    _, qkv_own, d_tokens, tokens_own, small_keep, small_send = attn_bwd(
        scal, qkv, probs, after(d_att, up[0]), d_tokens, w_qkv2[0], sums, tokens, 0, BLOCK, n_docs
    )

    def spread_small(small, stage, *before):
        pairs = [(d, d ^ (1 << stage)) for d in range(n_docs)]
        return after(small, *before) + lax.ppermute(small, "docs", pairs)

    down = stage_of(0, down, 2, qkv_own)
    lin = first_sum(0, [(after(qkv_own, down[0]), qkv_other)])
    up = stage_of(1, up, 1, lin[0])
    small = after(small_keep, up[0]) + swap(after(small_send, down[0]))
    lin = stage_of(0, lin, 0, small)
    d_tokens = place_other(scal, after(d_tokens, lin[0]), swap(after(tokens_own, down[0])), 2 * BLOCK)
    small = spread_small(small, 0, d_tokens)
    up = stage_of(1, up, 2, small)
    last = up[0]
    for stage in range(1, bits - 1):
        lin = stage_of(0, lin, stage, last)
        if stage + 2 < bits:
            down = stage_of(0, down, stage + 2, lin[0])
        if stage + 3 < bits:
            up = stage_of(1, up, stage + 2, down[0])
        if stage == bits - 2:
            up = stage_of(1, up, bits - 1, lin[0])
        small = spread_small(small, stage, up[0], down[0])
        last = small
    small = spread_small(small, bits - 1, up)
    lin = stage_of(0, lin, bits - 1, small)
    d_w_down = down.T
    d_w_up, d_w_out = up[:, :half], up[:, half:].T
    d_w_qkv = lin.reshape(-1, 3, cols)
    small = small.reshape(-1)
    width = tokens.shape[1]
    d_gain_two, d_shift_two, d_b_down, d_gain_one, d_shift_one, d_b_out = (
        small[i * width : (i + 1) * width] for i in range(6)
    )
    d_b_up = small[6 * width : 6 * width + half]
    d_b_qv = small[6 * width + half : 7 * width + half].reshape(2, cols)
    return (
        layer_out,
        d_tokens,
        d_w_qkv,
        d_b_qv,
        d_w_out,
        d_b_out,
        d_gain_one,
        d_shift_one,
        d_w_up,
        d_b_up,
        d_w_down,
        d_b_down,
        d_gain_two,
        d_shift_two,
    )


def solution(mesh):
    placed = (
        P("docs", None),
        P("docs", None),
        P("docs"),
        P(None, None, "heads"),
        P(None, "heads"),
        P("heads", None),
        P(),
        P(),
        P(),
        P(None, "heads"),
        P("heads"),
        P("heads", None),
        P(),
        P(),
        P(),
    )
    return jax.shard_map(
        functools.partial(shards, mesh.shape["docs"]),
        mesh=mesh,
        in_specs=placed,
        out_specs=(
            P("docs", None),
            P("docs", None),
            P("docs", None, "heads"),
            P(None, "heads"),
            P("heads", "docs"),
            P(),
            P(),
            P(),
            P("docs", "heads"),
            P("heads"),
            P("heads", "docs"),
            P(),
            P(),
            P(),
        ),
        check_vma=False,
    )
```

time: 866 us -> 196 us (0.23)
  waiting for transfers between devices: 512 us -> 29.2 us
  Pallas kernels: 0 us -> 116 us
  matrix products: 115 us -> 0 us
  blocking collectives: 77.7 us -> 0 us
  local copies, waits for them, and re-layouts: 82.7 us -> 6.88 us
  other arithmetic: 54.4 us -> 14.6 us
  starting transfers between devices: 0.58 us -> 27.2 us
  between operations: 15.9 us -> 1.6 us
    reduce_scatter x4 -> x0, waiting for transfers between devices: 437 us -> none  [the longest x1 142 us: shards(): lax.psum_scatter(d_w_up, 'docs', scatter_dimension=0, tiled=True)]
    pallas_call x0 -> x6, Pallas kernels: none -> 116 us  [the longest x1 34.9 us: ffn_fwd(): pl.pallas_call(functools.partial(ffn_fwd_kernel, block, rows, chunk, part...]
    dot_general x18 -> x0, matrix products: 115 us -> none  [the longest x4 40.7 us: left_dot(): lax.dot_general(first, second, (((0,), (0,)), ((), ())), preferred_elemen...]
    psum x1 -> x0, blocking collectives: 77.7 us -> none  [shards(): lax.psum((d_b_qv, d_b_out, d_gain_one, d_shift_one, d_b_up, d_b_down, d_g...]
    psum x4 -> x0, waiting for transfers between devices: 74.9 us -> none  [the longest x1 26 us: shards(): lax.psum(attn_part.astype(jnp.bfloat16), 'heads').astype(jnp.float32)]
    reduce_sum x11 -> x0, other arithmetic: 46.1 us -> none  [the longest x4 20.7 us: layer_norm(): center = values - jnp.mean(values, -1, keepdims=True)]
    ppermute x0 -> x29, waiting for transfers between devices: none -> 29.2 us  [the longest x13 12.3 us: swap(): return lax.ppermute(value, 'heads', [(0, 1), (1, 0)])]
    ppermute x0 -> x29, starting transfers between devices: none -> 27.2 us  [the longest x12 19.3 us: step(): return lax.ppermute(value, ('docs', 'heads'), pairs)]
  transfers between devices with their start and end apart: 8 -> 29, of which waited for: 7 -> 11; matrix products, arithmetic and copies ran while one was open for 7% -> 8% of each run, Pallas kernels for 0% -> 41%
where the time goes in v2:
time: 196 us; the launch traced here: 195 us
  Pallas kernels  116 us (59%)
  waiting for transfers between devices  29.2 us (15%)
  starting transfers between devices  27.2 us (14%)
  other arithmetic  14.6 us (7%)
  local copies, waits for them, and re-layouts  6.88 us (4%)
    pallas_call x1, Pallas kernels, ffn_fwd(): pl.pallas_call(functools.partial(ffn_fwd_kernel, block, rows, chunk, part...  34.9 us
    pallas_call x2, Pallas kernels, attn_bwd(): pl.pallas_call(functools.partial(attn_bwd_kernel, block, side, parts, ste...  31.7 us
    pallas_call x1, Pallas kernels, ffn_bwd(): pl.pallas_call(functools.partial(ffn_bwd_kernel, block, chunk, parts, ste...  31.7 us
    ppermute x12, starting transfers between devices, step(): return lax.ppermute(value, ('docs', 'heads'), pairs)  19.3 us
    pallas_call x1, Pallas kernels, attn_fwd(): pl.pallas_call(functools.partial(attn_fwd_kernel, block, rows), grid_spec...  13.9 us
    convert_element_type x13, other arithmetic, add(): return (left.astype(F32) + right.astype(F32)).astype(LOW)  12.4 us
    ppermute x13, waiting for transfers between devices, swap(): return lax.ppermute(value, 'heads', [(0, 1), (1, 0)])  12.3 us
    ppermute x12, waiting for transfers between devices, step(): return lax.ppermute(value, ('docs', 'heads'), pairs)  10.9 us
  transfers between devices with their start and end apart: 29, of which 11 were waited for; matrix products, arithmetic and copies ran while one was open for 8% of the time, Pallas kernels for 41%

profile of v2, /device:TPU:0, one launch (start us, length us, event | category | flops | bytes accessed | tf_op | source)
XLA Modules:
  0.0 195.2 jit_solution(17238780196036045046)
XLA Ops:
  1.7 3.0 %collective-permute-done.bt_ref = f32[2,384]{1,0:T(2,128)S(1)} collective-permute-done((f32[2,384]{1,0:T(2,128)}, f32[2,384]{1,0:T(2,128)S(1)}, u32[]{:S(2)}, u32[]{:S(2)}) %collective-permute-start) | collective-permute-done | bytes 3104 | tf_op jit(solution)/shard_map/ppermute | solution.py:590
  7.0 13.9 %attn_fwd.1 = (bf16[1024,2304]{1,0:T(8,128)(2,1)}, bf16[1024,1536]{1,0:T(8,128)(2,1)}, bf16[1024,768]{1,0:T(8,128)(2,1)}) custom-call(s32[66]{0:T(128)} %concatenate.9.s_ref, bf16[2048,768]{1,0:T(8,128)(2,1)} %refs_6_.3, f32[2,384]{1,0:T(2,128)} %bo_ref.2, f32[2,384]{1,0:T(2,128)} %copy-done.7, bf16[3,768,384]{2,1,0:T(8,128)(2,1)} %bitcast.25, ...), custom_call_target="tpu_custom_call" | custom-call | bytes 51660000 | tf_op jit(solution)/shard_map/attn_fwd/pallas_call | solution.py:165
  22.5 34.9 %ffn_fwd.1 = (f32[2048,768]{1,0:T(8,128)}, bf16[1024,768]{1,0:T(8,128)(2,1)}, bf16[1024,3072]{1,0:T(8,128)(2,1)}, bf16[1024,768]{1,0:T(8,128)(2,1)}, bf16[1024,7...) custom-call(s32[66]{0:T(128)} %concatenate.9.s_ref, ...), custom_call_target="tpu_custom_call" | custom-call | bytes 129150000 | tf_op jit(solution)/shard_map/ffn_fwd/pallas_call | solution.py:281
  57.6 4.6 %collective-permute-done.6 = bf16[16,48,1536]{2,1,0:T(8,128)(2,1)S(1)} collective-permute-done((bf16[16,48,1536]{2,1,0:T(8,128)(2,1)}, bf16[16,48,1536]{2,1,0:T(8,128)(2,1)S(1)}, u32[]{:S(2)}, u32[]{:S(2)}) %collective-permute-start.6) | collective-permute-done | bytes 2359328 | tf_op jit(solution)/shard_map/ppermute | solution.py:590
  62.2 2.3 %add_convert_fusion.2 = (bf16[8,48,1536]{2,1,0:T(8,128)(2,1)S(1)}, bf16[8,48,1536]{2,1,0:T(8,128)(2,1)S(1)}) fusion(bf16[16,48,1536]{2,1,0:T(8,128)(2,1)S(1)} %collective-permute-done.6, bf16[16,48,1536]{2,1,0:T(8,128)(2,1)} %get-tuple-element.84), kind=kLoop, calls=%fused_computation.2 | loop fusion | flops 4718592 | bytes 7077888 | tf_op jit(solution)/shard_map/convert_element_type | solution.py:619
  64.5 2.7 %collective-permute-start.7 = (bf16[8,48,1536]{2,1,0:T(8,128)(2,1)S(1)}, bf16[8,48,1536]{2,1,0:T(8,128)(2,1)S(1)}, u32[]{:S(2)}, u32[]{:S(2)}) collective-permute-start(bf16[8,48,1536]{2,1,0:T(8,128)(2,1)S(1)} %get-tuple-element.171), channel_id=1, source_target_pairs={{0,2},{1,5},{2,0},{3,7},{4,6},{5,1},{6,4},{7,3},{8,10},{9,13},{10,... | collective-permute-start | bytes 3538952 | tf_op jit(solution)/shard_map/ppermute | solution.py:587
  67.2 31.7 %ffn_bwd.1 = (f32[1024,768]{1,0:T(8,128)}, bf16[1024,768]{1,0:T(8,128)(2,1)}, f32[24,768]{1,0:T(8,128)}, f32[8,3072]{1,0:T(8,128)}, bf16[16,48,1536]{2,1,0:T(8,1...) custom-call(s32[66]{0:T(128)} %concatenate.9.s_ref, ...), custom_call_target="tpu_custom_call" | custom-call | bytes 118080000 | tf_op jit(solution)/shard_map/ffn_bwd/pallas_call | solution.py:395
  102.8 4.1 %collective-permute-done.9 = bf16[16,48,384]{2,1,0:T(8,128)(2,1)S(1)} collective-permute-done((bf16[16,48,384]{2,1,0:T(8,128)(2,1)}, bf16[16,48,384]{2,1,0:T(8,128)(2,1)S(1)}, u32[]{:S(2)}, u32[]{:S(2)}) %collective-permute-start.9) | collective-permute-done | bytes 589856 | tf_op jit(solution)/shard_map/ppermute | solution.py:590
  109.4 2.2 %collective-permute-start.12 = (bf16[8,48,1920]{2,1,0:T(8,128)(2,1)}, bf16[8,48,1920]{2,1,0:T(8,128)(2,1)}, u32[]{:S(2)}, u32[]{:S(2)}) collective-permute-start(bf16[8,48,1920]{2,1,0:T(8,128)(2,1)} %pad_maximum_fusion), channel_id=1, source_target_pairs={{0,2},{1,5},{2,0},{3,7},{4,6},{5,1},{6,4},{7,3},{8,10},{9,13},{10,... | collective-permute-start | bytes 4423688 | tf_op jit(solution)/shard_map/ppermute | solution.py:587
  111.7 15.9 %attn_bwd.2 = (f32[8,768]{1,0:T(8,128)}, bf16[16,48,1152]{2,1,0:T(8,128)(2,1)}, f32[1024,768]{1,0:T(8,128)}, f32[2048,768]{1,0:T(8,128)}) custom-call(s32[66]{0:T(128)} %concatenate.9.s_ref, bf16[1024,2304]{1,0:T(8,128)(2,1)} %get-tuple-element.77.refs_0_.refs_1_.refs_2_, ...), custom_call_target="tpu_custom_call", output_to_operand_aliasing={{3}: (10, {})} | custom-call | bytes 55350000 | tf_op jit(solution)/shard_map/attn_bwd/pallas_call | solution.py:528
  128.8 1.6 collective-permute-start.13
  130.3 2.6 %add_convert_fusion.6 = (bf16[4,48,1920]{2,1,0:T(8,128)(2,1)S(1)}, bf16[4,48,1920]{2,1,0:T(8,128)(2,1)}) fusion(bf16[8,48,1920]{2,1,0:T(8,128)(2,1)} %collective-permute-done.12, bf16[8,48,1920]{2,1,0:T(8,128)(2,1)S(1)} %pad_maximum_fusion.1), kind=kLoop, calls=%fused_computation.8 | loop fusion | flops 2949120 | bytes 4423680 | tf_op jit(solution)/shard_map/convert_element_type | solution.py:619
  134.1 15.8 %attn_bwd.3 = (f32[8,768]{1,0:T(8,128)}, bf16[16,48,1152]{2,1,0:T(8,128)(2,1)}, f32[2048,768]{1,0:T(8,128)}, bf16[1024,768]{1,0:T(8,128)(2,1)}, f32[56,128]{1,0:T(8,128)}, /*index=5*/f32[56,128]{1,0:T(8,128)}) custom-call(s32[66]{0:T(128)} %concatenate.9.s_ref, bf16[1024,2304]{1,0:T(8,128)(2,1)} %get-tuple-element.77.refs_0_.refs_1_.refs_2_, ...), custom_call_target="tpu_custom_call" | custom-call | bytes 55350000 | tf_op jit(solution)/shard_map/attn_bwd/pallas_call | solution.py:528
  151.1 1.9 add_convert_fusion.5
  154.0 2.6 %collective-permute-start.22 = (bf16[1,48,1536]{2,1,0:T(8,128)(2,1)S(1)}, bf16[1,48,1536]{2,1,0:T(8,128)(2,1)S(1)}, u32[]{:S(2)}, u32[]{:S(2)}) collective-permute-start(bf16[1,48,1536]{2,1,0:T(8,128)(2,1)S(1)} %get-tuple-element.191), channel_id=1, source_target_pairs={{0,16},{1,17},{2,18},{3,19},{4,20},{5,21},{6,22},{7,23},{8,24},{9,... | collective-permute-start | bytes 442376 | tf_op jit(solution)/shard_map/ppermute | solution.py:587
  158.8 1.8 collective-permute-start.19
  160.6 5.7 %collective-permute-done.17 = bf16[8,48,1152]{2,1,0:T(8,128)(2,1)S(1)} collective-permute-done((bf16[8,48,1152]{2,1,0:T(8,128)(2,1)S(1)}, bf16[8,48,1152]{2,1,0:T(8,128)(2,1)S(1)}, u32[]{:S(2)}, u32[]{:S(2)}) %collective-permute-start.17) | collective-permute-done | bytes 884768 | tf_op jit(solution)/shard_map/ppermute | solution.py:587
  167.5 3.6 %place_other.1 = f32[2048,768]{1,0:T(8,128)} custom-call(s32[66]{0:T(128)} %concatenate.9.s_ref, f32[2048,768]{1,0:T(8,128)} %get-tuple-element.127.whole_ref, bf16[1024,768]{1,0:T(8,128)(2,1)} %collective-permute-done.18.part_ref), custom_call_target="tpu_custom_call", output_to_operand_aliasing={{}: (1, {})} | custom-call | bytes 14760000 | tf_op jit(solution)/shard_map/place_other/pallas_call | solution.py:558
  172.4 2.8 %collective-permute-done.21 = bf16[4,48,1152]{2,1,0:T(8,128)(2,1)S(1)} collective-permute-done((bf16[4,48,1152]{2,1,0:T(8,128)(2,1)S(1)}, bf16[4,48,1152]{2,1,0:T(8,128)(2,1)S(1)}, u32[]{:S(2)}, u32[]{:S(2)}) %collective-permute-start.21) | collective-permute-done | bytes 442400 | tf_op jit(solution)/shard_map/ppermute | solution.py:587
  175.4 1.6 collective-permute-start.24
  178.3 2.6 %collective-permute-start.26 = (bf16[1,48,1920]{2,1,0:T(8,128)(2,1)S(1)}, bf16[1,48,1920]{2,1,0:T(8,128)(2,1)S(1)}, u32[]{:S(2)}, u32[]{:S(2)}) collective-permute-start(bf16[1,48,1920]{2,1,0:T(8,128)(2,1)S(1)} %get-tuple-element.189), channel_id=1, source_target_pairs={{0,16},{1,17},{2,18},{3,19},{4,20},{5,21},{6,22},{7,23},{8,24},{9,... | collective-permute-start | bytes 552968 | tf_op jit(solution)/shard_map/ppermute | solution.py:587
  180.9 4.2 %collective-permute-done.25 = f32[56,128]{1,0:T(8,128)S(1)} collective-permute-done((f32[56,128]{1,0:T(8,128)S(1)}, f32[56,128]{1,0:T(8,128)S(1)}, u32[]{:S(2)}, u32[]{:S(2)}) %collective-permute-start.25) | collective-permute-done | bytes 28704 | tf_op jit(solution)/shard_map/ppermute | solution.py:663
  186.5 1.5 collective-permute-done.26
  189.2 1.8 collective-permute-done.27
  (92 shorter events, 28.2 us)
Async XLA Ops:
  4.8 16.1 %collective-permute-start.4 = (bf16[768,1536]{1,0:T(8,128)(2,1)}, bf16[768,1536]{1,0:T(8,128)(2,1)S(1)}, u32[]{:S(2)}, u32[]{:S(2)}) collective-permute-start(bf16[768,1536]{1,0:T(8,128)(2,1)} %wuo_hbm.1), channel_id=1, source_target_pairs={{0,1},{1,0},{2,3},{3,2},{4,5},{5,4},{6,7},{7,6},{8,9},{9,8},{10,11... | collective-permute-start | bytes 7077896 | tf_op jit(solution)/shard_map/ppermute | solution.py:590
  5.2 15.7 %collective-permute-start.5 = (bf16[1536,768]{1,0:T(8,128)(2,1)}, bf16[1536,768]{1,0:T(8,128)(2,1)}, u32[]{:S(2)}, u32[]{:S(2)}) collective-permute-start(bf16[1536,768]{1,0:T(8,128)(2,1)} %wdo_hbm.1), channel_id=1, source_target_pairs={{0,1},{1,0},{2,3},{3,2},{4,5},{5,4},{6,7},{7,6},{8,9},{9,8},{10,11... | collective-permute-start | bytes 7077896 | tf_op jit(solution)/shard_map/ppermute | solution.py:590
  5.4 15.6 %collective-permute-start.3 = (bf16[384,768]{1,0:T(8,128)(2,1)}, bf16[384,768]{1,0:T(8,128)(2,1)S(1)}, u32[]{:S(2)}, u32[]{:S(2)}) collective-permute-start(bf16[384,768]{1,0:T(8,128)(2,1)} %woo_hbm.1), channel_id=1, source_target_pairs={{0,1},{1,0},{2,3},{3,2},{4,5},{5,4},{6,7},{7,6},{8,9},{9,8},{10,11... | collective-permute-start | bytes 1769480 | tf_op jit(solution)/shard_map/ppermute | solution.py:590
  64.5 34.4 %collective-permute-start.7 = (bf16[8,48,1536]{2,1,0:T(8,128)(2,1)S(1)}, bf16[8,48,1536]{2,1,0:T(8,128)(2,1)S(1)}, u32[]{:S(2)}, u32[]{:S(2)}) collective-permute-start(bf16[8,48,1536]{2,1,0:T(8,128)(2,1)S(1)} %get-tuple-element.171), channel_id=1, source_target_pairs={{0,2},{1,5},{2,0},{3,7},{4,6},{5,1},{6,4},{7,3},{8,10},{9,13},{10,... | collective-permute-start | bytes 3538952 | tf_op jit(solution)/shard_map/ppermute | solution.py:587
  100.8 6.7 %collective-permute-start.8 = (bf16[16,48,1536]{2,1,0:T(8,128)(2,1)S(1)}, bf16[16,48,1536]{2,1,0:T(8,128)(2,1)S(1)}, u32[]{:S(2)}, u32[]{:S(2)}) collective-permute-start(bf16[16,48,1536]{2,1,0:T(8,128)(2,1)S(1)} %copy-done.8), channel_id=1, source_target_pairs={{0,1},{1,0},{2,3},{3,2},{4,5},{5,4},{6,7},{7,6},{8,9},{9,8},{10,11... | collective-permute-start | bytes 7077896 | tf_op jit(solution)/shard_map/ppermute | solution.py:590
  100.9 6.1 %collective-permute-start.9 = (bf16[16,48,384]{2,1,0:T(8,128)(2,1)}, bf16[16,48,384]{2,1,0:T(8,128)(2,1)S(1)}, u32[]{:S(2)}, u32[]{:S(2)}) collective-permute-start(bf16[16,48,384]{2,1,0:T(8,128)(2,1)} %get-tuple-element.101), channel_id=1, source_target_pairs={{0,1},{1,0},{2,3},{3,2},{4,5},{5,4},{6,7},{7,6},{8,9},{9,8},{10,11... | collective-permute-start | bytes 1769480 | tf_op jit(solution)/shard_map/ppermute | solution.py:590
  101.3 10.4 %collective-permute-start.10 = (bf16[1024,768]{1,0:T(8,128)(2,1)}, bf16[1024,768]{1,0:T(8,128)(2,1)}, u32[]{:S(2)}, u32[]{:S(2)}) collective-permute-start(bf16[1024,768]{1,0:T(8,128)(2,1)} %get-tuple-element.104), channel_id=1, source_target_pairs={{0,1},{1,0},{2,3},{3,2},{4,5},{5,4},{6,7},{7,6},{8,9},{9,8},{10,11... | collective-permute-start | bytes 4718600 | tf_op jit(solution)/shard_map/ppermute | solution.py:590
  101.4 26.3 %collective-permute-start.11 = (bf16[4,48,1536]{2,1,0:T(8,128)(2,1)}, bf16[4,48,1536]{2,1,0:T(8,128)(2,1)S(1)}, u32[]{:S(2)}, u32[]{:S(2)}) collective-permute-start(bf16[4,48,1536]{2,1,0:T(8,128)(2,1)} %get-tuple-element.177), channel_id=1, source_target_pairs={{0,4},{1,3},{2,6},{3,1},{4,0},{5,7},{6,2},{7,5},{8,12},{9,11},{10,... | collective-permute-start | bytes 1769480 | tf_op jit(solution)/shard_map/ppermute | solution.py:587
  109.4 21.0 %collective-permute-start.12 = (bf16[8,48,1920]{2,1,0:T(8,128)(2,1)}, bf16[8,48,1920]{2,1,0:T(8,128)(2,1)}, u32[]{:S(2)}, u32[]{:S(2)}) collective-permute-start(bf16[8,48,1920]{2,1,0:T(8,128)(2,1)} %pad_maximum_fusion), channel_id=1, source_target_pairs={{0,2},{1,5},{2,0},{3,7},{4,6},{5,1},{6,4},{7,3},{8,10},{9,13},{10,... | collective-permute-start | bytes 4423688 | tf_op jit(solution)/shard_map/ppermute | solution.py:587
  128.6 22.4 %collective-permute-start.14 = (bf16[16,48,1152]{2,1,0:T(8,128)(2,1)}, bf16[16,48,1152]{2,1,0:T(8,128)(2,1)S(1)}, u32[]{:S(2)}, u32[]{:S(2)}) collective-permute-start(bf16[16,48,1152]{2,1,0:T(8,128)(2,1)} %get-tuple-element.120), channel_id=1, source_target_pairs={{0,1},{1,0},{2,3},{3,2},{4,5},{5,4},{6,7},{7,6},{8,9},{9,8},{10,11... | collective-permute-start | bytes 5308424 | tf_op jit(solution)/shard_map/ppermute | solution.py:590
  128.8 21.1 %collective-permute-start.13 = (bf16[2,48,1536]{2,1,0:T(8,128)(2,1)}, bf16[2,48,1536]{2,1,0:T(8,128)(2,1)}, u32[]{:S(2)}, u32[]{:S(2)}) collective-permute-start(bf16[2,48,1536]{2,1,0:T(8,128)(2,1)} %get-tuple-element.183), channel_id=1, source_target_pairs={{0,8},{1,9},{2,10},{3,11},{4,12},{5,13},{6,14},{7,15},{8,0},{9,1},... | collective-permute-start | bytes 884744 | tf_op jit(solution)/shard_map/ppermute | solution.py:587
  132.9 23.7 %collective-permute-start.15 = (bf16[4,48,1920]{2,1,0:T(8,128)(2,1)}, bf16[4,48,1920]{2,1,0:T(8,128)(2,1)}, u32[]{:S(2)}, u32[]{:S(2)}) collective-permute-start(bf16[4,48,1920]{2,1,0:T(8,128)(2,1)} %get-tuple-element.175), channel_id=1, source_target_pairs={{0,4},{1,3},{2,6},{3,1},{4,0},{5,7},{6,2},{7,5},{8,12},{9,11},{10,... | collective-permute-start | bytes 2211848 | tf_op jit(solution)/shard_map/ppermute | solution.py:587
  151.0 16.6 %collective-permute-start.18 = (bf16[1024,768]{1,0:T(8,128)(2,1)}, bf16[1024,768]{1,0:T(8,128)(2,1)}, u32[]{:S(2)}, u32[]{:S(2)}) collective-permute-start(bf16[1024,768]{1,0:T(8,128)(2,1)} %get-tuple-element.129), channel_id=1, source_target_pairs={{0,1},{1,0},{2,3},{3,2},{4,5},{5,4},{6,7},{7,6},{8,9},{9,8},{10,11... | collective-permute-start | bytes 4718600 | tf_op jit(solution)/shard_map/ppermute | solution.py:590
  152.9 13.4 %collective-permute-start.17 = (bf16[8,48,1152]{2,1,0:T(8,128)(2,1)S(1)}, bf16[8,48,1152]{2,1,0:T(8,128)(2,1)S(1)}, u32[]{:S(2)}, u32[]{:S(2)}) collective-permute-start(bf16[8,48,1152]{2,1,0:T(8,128)(2,1)S(1)} %get-tuple-element.173), channel_id=1, source_target_pairs={{0,2},{1,5},{2,0},{3,7},{4,6},{5,1},{6,4},{7,3},{8,10},{9,13},{10,... | collective-permute-start | bytes 2654216 | tf_op jit(solution)/shard_map/ppermute | solution.py:587
  154.0 23.0 %collective-permute-start.22 = (bf16[1,48,1536]{2,1,0:T(8,128)(2,1)S(1)}, bf16[1,48,1536]{2,1,0:T(8,128)(2,1)S(1)}, u32[]{:S(2)}, u32[]{:S(2)}) collective-permute-start(bf16[1,48,1536]{2,1,0:T(8,128)(2,1)S(1)} %get-tuple-element.191), channel_id=1, source_target_pairs={{0,16},{1,17},{2,18},{3,19},{4,20},{5,21},{6,22},{7,23},{8,24},{9,... | collective-permute-start | bytes 442376 | tf_op jit(solution)/shard_map/ppermute | solution.py:587
  157.9 14.5 %collective-permute-start.20 = (bf16[2,48,1920]{2,1,0:T(8,128)(2,1)S(1)}, bf16[2,48,1920]{2,1,0:T(8,128)(2,1)S(1)}, u32[]{:S(2)}, u32[]{:S(2)}) collective-permute-start(bf16[2,48,1920]{2,1,0:T(8,128)(2,1)S(1)} %get-tuple-element.181), channel_id=1, source_target_pairs={{0,8},{1,9},{2,10},{3,11},{4,12},{5,13},{6,14},{7,15},{8,0},{9,1},... | collective-permute-start | bytes 1105928 | tf_op jit(solution)/shard_map/ppermute | solution.py:587
  158.8 12.3 %collective-permute-start.19 = (f32[56,128]{1,0:T(8,128)S(1)}, f32[56,128]{1,0:T(8,128)S(1)}, u32[]{:S(2)}, u32[]{:S(2)}) collective-permute-start(f32[56,128]{1,0:T(8,128)S(1)} %add.118), channel_id=1, source_target_pairs={{0,2},{2,0},{4,6},{6,4},{8,10},{10,8},{12,14},{14,12},{16,18},{18,... | collective-permute-start | bytes 86024 | tf_op jit(solution)/shard_map/ppermute | solution.py:663
  166.6 8.7 %collective-permute-start.21 = (bf16[4,48,1152]{2,1,0:T(8,128)(2,1)S(1)}, bf16[4,48,1152]{2,1,0:T(8,128)(2,1)S(1)}, u32[]{:S(2)}, u32[]{:S(2)}) collective-permute-start(bf16[4,48,1152]{2,1,0:T(8,128)(2,1)S(1)} %get-tuple-element.179), channel_id=1, source_target_pairs={{0,4},{1,3},{2,6},{3,1},{4,0},{5,7},{6,2},{7,5},{8,12},{9,11},{10,... | collective-permute-start | bytes 1327112 | tf_op jit(solution)/shard_map/ppermute | solution.py:587
  171.1 6.6 %collective-permute-start.23 = (f32[56,128]{1,0:T(8,128)S(1)}, f32[56,128]{1,0:T(8,128)S(1)}, u32[]{:S(2)}, u32[]{:S(2)}) collective-permute-start(f32[56,128]{1,0:T(8,128)S(1)} %add.122), channel_id=1, source_target_pairs={{0,4},{2,6},{4,0},{6,2},{8,12},{10,14},{12,8},{14,10},{16,20},{18,... | collective-permute-start | bytes 86024 | tf_op jit(solution)/shard_map/ppermute | solution.py:663
  175.4 11.1 %collective-permute-start.24 = (bf16[2,48,1152]{2,1,0:T(8,128)(2,1)S(1)}, bf16[2,48,1152]{2,1,0:T(8,128)(2,1)S(1)}, u32[]{:S(2)}, u32[]{:S(2)}) collective-permute-start(bf16[2,48,1152]{2,1,0:T(8,128)(2,1)S(1)} %get-tuple-element.187), channel_id=1, source_target_pairs={{0,8},{1,9},{2,10},{3,11},{4,12},{5,13},{6,14},{7,15},{8,0},{9,1},... | collective-permute-start | bytes 663560 | tf_op jit(solution)/shard_map/ppermute | solution.py:587
  177.8 7.3 %collective-permute-start.25 = (f32[56,128]{1,0:T(8,128)S(1)}, f32[56,128]{1,0:T(8,128)S(1)}, u32[]{:S(2)}, u32[]{:S(2)}) collective-permute-start(f32[56,128]{1,0:T(8,128)S(1)} %add.128), channel_id=1, source_target_pairs={{0,8},{2,10},{4,12},{6,14},{8,0},{10,2},{12,4},{14,6},{16,24},{18,... | collective-permute-start | bytes 86024 | tf_op jit(solution)/shard_map/ppermute | solution.py:663
  178.3 9.7 %collective-permute-start.26 = (bf16[1,48,1920]{2,1,0:T(8,128)(2,1)S(1)}, bf16[1,48,1920]{2,1,0:T(8,128)(2,1)S(1)}, u32[]{:S(2)}, u32[]{:S(2)}) collective-permute-start(bf16[1,48,1920]{2,1,0:T(8,128)(2,1)S(1)} %get-tuple-element.189), channel_id=1, source_target_pairs={{0,16},{1,17},{2,18},{3,19},{4,20},{5,21},{6,22},{7,23},{8,24},{9,... | collective-permute-start | bytes 552968 | tf_op jit(solution)/shard_map/ppermute | solution.py:587
  185.1 5.9 %collective-permute-start.27 = (f32[56,128]{1,0:T(8,128)S(1)}, f32[56,128]{1,0:T(8,128)S(1)}, u32[]{:S(2)}, u32[]{:S(2)}) collective-permute-start(f32[56,128]{1,0:T(8,128)S(1)} %add.130), channel_id=1, source_target_pairs={{0,16},{2,18},{4,20},{6,22},{8,24},{10,26},{12,28},{14,30},{16,0},... | collective-permute-start | bytes 86024 | tf_op jit(solution)/shard_map/ppermute | solution.py:663
  188.7 5.6 %collective-permute-start.28 = (bf16[1,48,1152]{2,1,0:T(8,128)(2,1)S(1)}, bf16[1,48,1152]{2,1,0:T(8,128)(2,1)S(1)}, u32[]{:S(2)}, u32[]{:S(2)}) collective-permute-start(bf16[1,48,1152]{2,1,0:T(8,128)(2,1)S(1)} %get-tuple-element.193), channel_id=1, source_target_pairs={{0,16},{1,17},{2,18},{3,19},{4,20},{5,21},{6,22},{7,23},{8,24},{9,... | collective-permute-start | bytes 331784 | tf_op jit(solution)/shard_map/ppermute | solution.py:587
  (15 other events, 84.9 us)

commit v3 on v2

--- a/solution.py
+++ b/solution.py
@@ -14,9 +14,9 @@
 F32 = jnp.float32
 LOW = jnp.bfloat16
 OWN = jnp.bfloat16
-FF_CHUNK = 768
+FF_CHUNK = 1536
 BLOCK = 256
-VMEM_LIMIT = 60 * 1024 * 1024
+MIB = 1024 * 1024
 
 
 def mm(first, second):
@@ -55,8 +55,8 @@
     return pl.CostEstimate(flops=0, bytes_accessed=int(micros * 3.69e6), transcendentals=0)
 
 
-def params():
-    return pltpu.CompilerParams(dimension_semantics=("arbitrary",), vmem_limit_bytes=VMEM_LIMIT)
+def params(mebibytes):
+    return pltpu.CompilerParams(dimension_semantics=("arbitrary",), vmem_limit_bytes=mebibytes * MIB)
 
 
 def slots_of(width, parts):
@@ -174,7 +174,7 @@
             scratch_shapes=[pltpu.VMEM((width, 6 * cols), LOW), pltpu.SemaphoreType.DMA((6,))],
         ),
         out_shape=[jax.ShapeDtypeStruct((rows, w), LOW) for w in outs],
-        compiler_params=params(),
+        compiler_params=params(60),
         cost_estimate=cost(14),
         name="attn_fwd",
     )(scal, tokens, *b, *w)
@@ -302,7 +302,7 @@
         + [jax.ShapeDtypeStruct((rows, w), t) for w, t in outs]
         + [jax.ShapeDtypeStruct((24, width), F32)]
         + [jax.ShapeDtypeStruct((*lead, half), LOW)] * 2,
-        compiler_params=params(),
+        compiler_params=params(50),
         cost_estimate=cost(35),
         name="ffn_fwd",
     )(scal, tokens, grad_out, att, *small, *weights)
@@ -420,7 +420,7 @@
         ]
         + [jax.ShapeDtypeStruct((*lead, half), LOW)] * 2
         + [jax.ShapeDtypeStruct((*lead, cols), LOW)] * 2,
-        compiler_params=params(),
+        compiler_params=params(48),
         cost_estimate=cost(32),
         name="ffn_bwd",
     )(scal, *moving, gain_one, *w_out, *w_up, *w_down, normed_low, att)
@@ -542,7 +542,7 @@
         ),
         out_shape=out_shape,
         input_output_aliases={10: 3} if side else {},
-        compiler_params=params(),
+        compiler_params=params(30),
         cost_estimate=cost(15),
         name="attn_bwd",
     )(scal, qkv, qkv, qkv, probs, d_att, base, tokens, w, *extra)
@@ -565,7 +565,7 @@
         ),
         out_shape=jax.ShapeDtypeStruct(whole.shape, F32),
         input_output_aliases={1: 0},
-        compiler_params=params(),
+        compiler_params=params(16),
         cost_estimate=cost(4),
         name="place_other",
     )(scal, whole, piece)
@@ -609,7 +609,7 @@
     w_qkv2 = (w_qkv, swap(w_qkv))
     b_qv2 = (b_qv, swap(b_qv))
     b_up2 = (b_up, swap(b_up))
-    w_out, w_up, w_down = after((w_out, w_up, w_down), w_qkv2[1], b_qv2[1], b_up2[1])
+    w_out, w_up, w_down = after((w_out, w_up, w_down), w_qkv2[1], b_qv2[1], b_up2[1], scal)
     w_out2 = (w_out, swap(w_out))
     w_up2 = (w_up, swap(w_up))
     w_down2 = (w_down, swap(w_down))
@@ -645,7 +645,7 @@
         scal, d_mlp, slope, hat, scale, normed_low, att, w_out2, w_up2, w_down2, gain_one, BLOCK, FF_CHUNK, 768, n_docs
     )
     down = stage_of(0, down, 0, up_own)
-    up_own, up_other, out_own, out_other, layer_own = after((up_own, up_other, out_own, out_other, layer_own), down[0])
+    up_own, out_own, out_other, layer_own = after((up_own, out_own, out_other, layer_own), down[0])
     up = first_sum(1, [(up_own, up_other), (out_own, out_other)])
     sums_other, qkv_other, d_tokens, layer_out = attn_bwd(
         scal, qkv, probs, after(d_att, *up), d_h1, w_qkv2[1], (swap(layer_own), layer_out), tokens, 1, BLOCK, n_docs

time: 196 us -> 178 us (0.908)
  Pallas kernels: 116 us -> 107 us
  other arithmetic: 14.6 us -> 6.55 us
    convert_element_type x13, other arithmetic: 12.4 us -> 5.49 us  [add(): return (left.astype(F32) + right.astype(F32)).astype(LOW)]
    pallas_call x2, Pallas kernels: 31.7 us -> 27.5 us  [attn_bwd(): pl.pallas_call(functools.partial(attn_bwd_kernel, block, side, parts, ste...]
    ppermute x12, waiting for transfers between devices: 10.9 us -> 14.4 us  [step(): return lax.ppermute(value, ('docs', 'heads'), pairs)]
    ppermute x13, waiting for transfers between devices: 12.3 us -> 8.96 us  [swap(): return lax.ppermute(value, 'heads', [(0, 1), (1, 0)])]
  transfers between devices with their start and end apart: 29 -> 29, of which waited for: 11 -> 9; matrix products, arithmetic and copies ran while one was open for 8% -> 4% of each run, Pallas kernels for 41% -> 41%
where the time goes in v3:
time: 178 us
  Pallas kernels  107 us (60%)
  waiting for transfers between devices  28.5 us (16%)
  starting transfers between devices  26.9 us (15%)
  local copies, waits for them, and re-layouts  7.59 us (4%)
  other arithmetic  6.55 us (4%)
    pallas_call x1, Pallas kernels, ffn_fwd(): pl.pallas_call(functools.partial(ffn_fwd_kernel, block, rows, chunk, part...  33 us
    pallas_call x1, Pallas kernels, ffn_bwd(): pl.pallas_call(functools.partial(ffn_bwd_kernel, block, chunk, parts, ste...  30.3 us
    pallas_call x2, Pallas kernels, attn_bwd(): pl.pallas_call(functools.partial(attn_bwd_kernel, block, side, parts, ste...  27.5 us
    ppermute x12, starting transfers between devices, step(): return lax.ppermute(value, ('docs', 'heads'), pairs)  18.5 us
    ppermute x12, waiting for transfers between devices, step(): return lax.ppermute(value, ('docs', 'heads'), pairs)  14.4 us
    pallas_call x1, Pallas kernels, attn_fwd(): pl.pallas_call(functools.partial(attn_fwd_kernel, block, rows), grid_spec...  13.9 us
    ppermute x13, waiting for transfers between devices, swap(): return lax.ppermute(value, 'heads', [(0, 1), (1, 0)])  8.96 us
    convert_element_type x13, other arithmetic, add(): return (left.astype(F32) + right.astype(F32)).astype(LOW)  5.49 us
  transfers between devices with their start and end apart: 29, of which 9 were waited for; matrix products, arithmetic and copies ran while one was open for 4% of the time, Pallas kernels for 41%

profile of v3, /device:TPU:0, one launch (start us, length us, event | category | flops | bytes accessed | tf_op | source)
XLA Modules:
  0.0 178.3 jit_solution(15425116674496915324)
XLA Ops:
  3.0 1.7 collective-permute-done.bt_ref
  6.0 13.9 %attn_fwd.1 = (bf16[1024,2304]{1,0:T(8,128)(2,1)}, bf16[1024,1536]{1,0:T(8,128)(2,1)}, bf16[1024,768]{1,0:T(8,128)(2,1)}) custom-call(s32[66]{0:T(128)} %concatenate.9.s_ref, bf16[2048,768]{1,0:T(8,128)(2,1)} %refs_6_.3, f32[2,384]{1,0:T(2,128)} %bo_ref.2, f32[2,384]{1,0:T(2,128)} %copy-done.17, bf16[3,768,384]{2,1,0:T(8,128)(2,1)} %bitcast.27, ...), custom_call_target="tpu_custom_call" | custom-call | bytes 51660000 | tf_op jit(solution)/shard_map/attn_fwd/pallas_call | solution.py:165
  20.0 33.0 %ffn_fwd.1 = (f32[2048,768]{1,0:T(8,128)}, bf16[1024,768]{1,0:T(8,128)(2,1)S(1)}, bf16[1024,3072]{1,0:T(8,128)(2,1)}, bf16[1024,768]{1,0:T(8,128)(2,1)}, bf16[10...) custom-call(s32[66]{0:T(128)S(1)} %copy-done.8, ...), custom_call_target="tpu_custom_call" | custom-call | bytes 129150000 | tf_op jit(solution)/shard_map/ffn_fwd/pallas_call | solution.py:281
  53.5 4.4 %collective-permute-done.6 = bf16[16,48,1536]{2,1,0:T(8,128)(2,1)S(1)} collective-permute-done((bf16[16,48,1536]{2,1,0:T(8,128)(2,1)}, bf16[16,48,1536]{2,1,0:T(8,128)(2,1)S(1)}, u32[]{:S(2)}, u32[]{:S(2)}) %collective-permute-start.6) | collective-permute-done | bytes 2359328 | tf_op jit(solution)/shard_map/ppermute | solution.py:590
  57.8 2.6 %add_convert_fusion.2 = (bf16[8,48,1536]{2,1,0:T(8,128)(2,1)S(1)}, bf16[8,48,1536]{2,1,0:T(8,128)(2,1)S(1)}) fusion(bf16[16,48,1536]{2,1,0:T(8,128)(2,1)S(1)} %collective-permute-done.6, bf16[16,48,1536]{2,1,0:T(8,128)(2,1)} %get-tuple-element.83), kind=kLoop, calls=%fused_computation.2 | loop fusion | flops 4718592 | bytes 7077888 | tf_op jit(solution)/shard_map/convert_element_type | solution.py:619
  60.4 2.9 %collective-permute-start.7 = (bf16[8,48,1536]{2,1,0:T(8,128)(2,1)S(1)}, bf16[8,48,1536]{2,1,0:T(8,128)(2,1)S(1)}, u32[]{:S(2)}, u32[]{:S(2)}) collective-permute-start(bf16[8,48,1536]{2,1,0:T(8,128)(2,1)S(1)} %get-tuple-element.169), channel_id=1, source_target_pairs={{0,2},{1,5},{2,0},{3,7},{4,6},{5,1},{6,4},{7,3},{8,10},{9,13},{10,... | collective-permute-start | bytes 3538952 | tf_op jit(solution)/shard_map/ppermute | solution.py:587
  63.3 30.3 %ffn_bwd.1 = (f32[1024,768]{1,0:T(8,128)}, bf16[1024,768]{1,0:T(8,128)(2,1)S(1)}, f32[24,768]{1,0:T(8,128)S(1)}, f32[8,3072]{1,0:T(8,128)S(1)}, bf16[16,48,1536]...) custom-call(s32[66]{0:T(128)S(1)} %copy-done.8, ...), custom_call_target="tpu_custom_call" | custom-call | bytes 118080000 | tf_op jit(solution)/shard_map/ffn_bwd/pallas_call | solution.py:395
  94.6 1.5 collective-permute-start.11
  96.2 2.9 %collective-permute-done.9 = bf16[16,48,384]{2,1,0:T(8,128)(2,1)S(1)} collective-permute-done((bf16[16,48,384]{2,1,0:T(8,128)(2,1)S(1)}, bf16[16,48,384]{2,1,0:T(8,128)(2,1)S(1)}, u32[]{:S(2)}, u32[]{:S(2)}) %collective-permute-start.9) | collective-permute-done | bytes 589856 | tf_op jit(solution)/shard_map/ppermute | solution.py:590
  104.0 13.9 %attn_bwd.2 = (f32[8,768]{1,0:T(8,128)S(1)}, bf16[16,48,1152]{2,1,0:T(8,128)(2,1)S(1)}, f32[1024,768]{1,0:T(8,128)S(1)}, f32[2048,768]{1,0:T(8,128)}) custom-call(s32[66]{0:T(128)S(1)} %copy-done.8, bf16[1024,2304]{1,0:T(8,128)(2,1)S(1)} %bitcast.25, bf16[1024,2304]{1,0:T(8,128)(2,1)S(1)} %bitcast.25, ...), custom_call_target="tpu_custom_call", output_to_operand_aliasing={{3}: (10, {})} | custom-call | bytes 55350000 | tf_op jit(solution)/shard_map/attn_bwd/pallas_call | solution.py:528
  118.3 1.6 collective-permute-start.13
  120.2 1.6 collective-permute-start.15
  121.8 13.6 %attn_bwd.3 = (f32[8,768]{1,0:T(8,128)}, bf16[16,48,1152]{2,1,0:T(8,128)(2,1)S(1)}, f32[2048,768]{1,0:T(8,128)}, bf16[1024,768]{1,0:T(8,128)(2,1)S(1)}, f32[56,128]{1,0:T(8,128)S(1)}, /*index=5*/f32[56,128]{1,0:T(8,128)S(1)}) custom-call(s32[66]{0:T(128)S(1)} %copy-done.8, bf16[1024,2304]{1,0:T(8,128)(2,1)S(1)} %bitcast.25, bf16[1024,2304]{1,0:T(8,128)(2,1)S(1)} %bitcast.25, ...), custom_call_target="tpu_custom_call" | custom-call | bytes 55350000 | tf_op jit(solution)/shard_map/attn_bwd/pallas_call | solution.py:528
  136.7 2.6 %collective-permute-start.22 = (bf16[1,48,1536]{2,1,0:T(8,128)(2,1)S(1)}, bf16[1,48,1536]{2,1,0:T(8,128)(2,1)S(1)}, u32[]{:S(2)}, u32[]{:S(2)}) collective-permute-start(bf16[1,48,1536]{2,1,0:T(8,128)(2,1)S(1)} %get-tuple-element.189), channel_id=1, source_target_pairs={{0,16},{1,17},{2,18},{3,19},{4,20},{5,21},{6,22},{7,23},{8,24},{9,... | collective-permute-start | bytes 442376 | tf_op jit(solution)/shard_map/ppermute | solution.py:587
  139.4 1.6 collective-permute-start.20
  141.0 1.5 collective-permute-start.19
  142.6 6.9 %collective-permute-done.17 = bf16[8,48,1152]{2,1,0:T(8,128)(2,1)S(1)} collective-permute-done((bf16[8,48,1152]{2,1,0:T(8,128)(2,1)S(1)}, bf16[8,48,1152]{2,1,0:T(8,128)(2,1)S(1)}, u32[]{:S(2)}, u32[]{:S(2)}) %collective-permute-start.17) | collective-permute-done | bytes 884768 | tf_op jit(solution)/shard_map/ppermute | solution.py:587
  150.3 2.3 %place_other.1 = f32[2048,768]{1,0:T(8,128)} custom-call(s32[66]{0:T(128)S(1)} %copy-done.8, f32[2048,768]{1,0:T(8,128)} %get-tuple-element.125.whole_ref, bf16[1024,768]{1,0:T(8,128)(2,1)S(1)} %collective-permute-done.18.part_ref), custom_call_target="tpu_custom_call", output_to_operand_aliasing={{}: (1, {})} | custom-call | bytes 14760000 | tf_op jit(solution)/shard_map/place_other/pallas_call | solution.py:558
  152.6 1.6 collective-permute-start.23
  154.3 4.1 %collective-permute-done.21 = bf16[4,48,1152]{2,1,0:T(8,128)(2,1)S(1)} collective-permute-done((bf16[4,48,1152]{2,1,0:T(8,128)(2,1)S(1)}, bf16[4,48,1152]{2,1,0:T(8,128)(2,1)S(1)}, u32[]{:S(2)}, u32[]{:S(2)}) %collective-permute-start.21) | collective-permute-done | bytes 442400 | tf_op jit(solution)/shard_map/ppermute | solution.py:587
  158.5 1.6 collective-permute-start.24
  161.4 2.6 %collective-permute-start.26 = (bf16[1,48,1920]{2,1,0:T(8,128)(2,1)S(1)}, bf16[1,48,1920]{2,1,0:T(8,128)(2,1)S(1)}, u32[]{:S(2)}, u32[]{:S(2)}) collective-permute-start(bf16[1,48,1920]{2,1,0:T(8,128)(2,1)S(1)} %get-tuple-element.187), channel_id=1, source_target_pairs={{0,16},{1,17},{2,18},{3,19},{4,20},{5,21},{6,22},{7,23},{8,24},{9,... | collective-permute-start | bytes 552968 | tf_op jit(solution)/shard_map/ppermute | solution.py:587
  164.0 4.2 %collective-permute-done.25 = f32[56,128]{1,0:T(8,128)S(1)} collective-permute-done((f32[56,128]{1,0:T(8,128)S(1)}, f32[56,128]{1,0:T(8,128)S(1)}, u32[]{:S(2)}, u32[]{:S(2)}) %collective-permute-start.25) | collective-permute-done | bytes 28704 | tf_op jit(solution)/shard_map/ppermute | solution.py:663
  175.5 1.9 %collective-permute-done.28 = bf16[1,48,1152]{2,1,0:T(8,128)(2,1)S(1)} collective-permute-done((bf16[1,48,1152]{2,1,0:T(8,128)(2,1)S(1)}, bf16[1,48,1152]{2,1,0:T(8,128)(2,1)S(1)}, u32[]{:S(2)}, u32[]{:S(2)}) %collective-permute-start.28) | collective-permute-done | bytes 110624 | tf_op jit(solution)/shard_map/ppermute | solution.py:587
  (113 shorter events, 21.9 us)
Async XLA Ops:
  4.7 15.2 %collective-permute-start.4 = (bf16[768,1536]{1,0:T(8,128)(2,1)}, bf16[768,1536]{1,0:T(8,128)(2,1)}, u32[]{:S(2)}, u32[]{:S(2)}) collective-permute-start(bf16[768,1536]{1,0:T(8,128)(2,1)} %wuo_hbm.1), channel_id=1, source_target_pairs={{0,1},{1,0},{2,3},{3,2},{4,5},{5,4},{6,7},{7,6},{8,9},{9,8},{10,11... | collective-permute-start | bytes 7077896 | tf_op jit(solution)/shard_map/ppermute | solution.py:590
  5.2 14.7 %collective-permute-start.5 = (bf16[1536,768]{1,0:T(8,128)(2,1)}, bf16[1536,768]{1,0:T(8,128)(2,1)}, u32[]{:S(2)}, u32[]{:S(2)}) collective-permute-start(bf16[1536,768]{1,0:T(8,128)(2,1)} %wdo_hbm.1), channel_id=1, source_target_pairs={{0,1},{1,0},{2,3},{3,2},{4,5},{5,4},{6,7},{7,6},{8,9},{9,8},{10,11... | collective-permute-start | bytes 7077896 | tf_op jit(solution)/shard_map/ppermute | solution.py:590
  5.3 14.6 %collective-permute-start.3 = (bf16[384,768]{1,0:T(8,128)(2,1)}, bf16[384,768]{1,0:T(8,128)(2,1)S(1)}, u32[]{:S(2)}, u32[]{:S(2)}) collective-permute-start(bf16[384,768]{1,0:T(8,128)(2,1)} %woo_hbm.1), channel_id=1, source_target_pairs={{0,1},{1,0},{2,3},{3,2},{4,5},{5,4},{6,7},{7,6},{8,9},{9,8},{10,11... | collective-permute-start | bytes 1769480 | tf_op jit(solution)/shard_map/ppermute | solution.py:590
  53.0 4.8 %collective-permute-start.6 = (bf16[16,48,1536]{2,1,0:T(8,128)(2,1)}, bf16[16,48,1536]{2,1,0:T(8,128)(2,1)S(1)}, u32[]{:S(2)}, u32[]{:S(2)}) collective-permute-start(bf16[16,48,1536]{2,1,0:T(8,128)(2,1)} %get-tuple-element.84), channel_id=1, source_target_pairs={{0,1},{1,0},{2,3},{3,2},{4,5},{5,4},{6,7},{7,6},{8,9},{9,8},{10,11... | collective-permute-start | bytes 7077896 | tf_op jit(solution)/shard_map/ppermute | solution.py:590
  60.4 33.3 %collective-permute-start.7 = (bf16[8,48,1536]{2,1,0:T(8,128)(2,1)S(1)}, bf16[8,48,1536]{2,1,0:T(8,128)(2,1)S(1)}, u32[]{:S(2)}, u32[]{:S(2)}) collective-permute-start(bf16[8,48,1536]{2,1,0:T(8,128)(2,1)S(1)} %get-tuple-element.169), channel_id=1, source_target_pairs={{0,2},{1,5},{2,0},{3,7},{4,6},{5,1},{6,4},{7,3},{8,10},{9,13},{10,... | collective-permute-start | bytes 3538952 | tf_op jit(solution)/shard_map/ppermute | solution.py:587
  93.6 5.6 %collective-permute-start.8 = (bf16[16,48,1536]{2,1,0:T(8,128)(2,1)}, bf16[16,48,1536]{2,1,0:T(8,128)(2,1)S(1)}, u32[]{:S(2)}, u32[]{:S(2)}) collective-permute-start(bf16[16,48,1536]{2,1,0:T(8,128)(2,1)} %get-tuple-element.97), channel_id=1, source_target_pairs={{0,1},{1,0},{2,3},{3,2},{4,5},{5,4},{6,7},{7,6},{8,9},{9,8},{10,11... | collective-permute-start | bytes 7077896 | tf_op jit(solution)/shard_map/ppermute | solution.py:590
  94.0 5.0 %collective-permute-start.9 = (bf16[16,48,384]{2,1,0:T(8,128)(2,1)S(1)}, bf16[16,48,384]{2,1,0:T(8,128)(2,1)S(1)}, u32[]{:S(2)}, u32[]{:S(2)}) collective-permute-start(bf16[16,48,384]{2,1,0:T(8,128)(2,1)S(1)} %get-tuple-element.99), channel_id=1, source_target_pairs={{0,1},{1,0},{2,3},{3,2},{4,5},{5,4},{6,7},{7,6},{8,9},{9,8},{10,11... | collective-permute-start | bytes 1769480 | tf_op jit(solution)/shard_map/ppermute | solution.py:590
  94.6 6.7 %collective-permute-start.10 = (bf16[1024,768]{1,0:T(8,128)(2,1)S(1)}, bf16[1024,768]{1,0:T(8,128)(2,1)S(1)}, u32[]{:S(2)}, u32[]{:S(2)}) collective-permute-start(bf16[1024,768]{1,0:T(8,128)(2,1)S(1)} %get-tuple-element.102), channel_id=1, source_target_pairs={{0,1},{1,0},{2,3},{3,2},{4,5},{5,4},{6,7},{7,6},{8,9},{9,8},{10,11... | collective-permute-start | bytes 4718600 | tf_op jit(solution)/shard_map/ppermute | solution.py:590
  94.6 23.3 %collective-permute-start.11 = (bf16[4,48,1536]{2,1,0:T(8,128)(2,1)S(1)}, bf16[4,48,1536]{2,1,0:T(8,128)(2,1)S(1)}, u32[]{:S(2)}, u32[]{:S(2)}) collective-permute-start(bf16[4,48,1536]{2,1,0:T(8,128)(2,1)S(1)} %get-tuple-element.175), channel_id=1, source_target_pairs={{0,4},{1,3},{2,6},{3,1},{4,0},{5,7},{6,2},{7,5},{8,12},{9,11},{10,... | collective-permute-start | bytes 1769480 | tf_op jit(solution)/shard_map/ppermute | solution.py:587
  100.1 19.8 %collective-permute-start.12 = (bf16[8,48,1920]{2,1,0:T(8,128)(2,1)S(1)}, bf16[8,48,1920]{2,1,0:T(8,128)(2,1)S(1)}, u32[]{:S(2)}, u32[]{:S(2)}) collective-permute-start(bf16[8,48,1920]{2,1,0:T(8,128)(2,1)S(1)} %pad_maximum_fusion), channel_id=1, source_target_pairs={{0,2},{1,5},{2,0},{3,7},{4,6},{5,1},{6,4},{7,3},{8,10},{9,13},{10,... | collective-permute-start | bytes 4423688 | tf_op jit(solution)/shard_map/ppermute | solution.py:587
  118.1 17.5 %collective-permute-start.14 = (bf16[16,48,1152]{2,1,0:T(8,128)(2,1)S(1)}, bf16[16,48,1152]{2,1,0:T(8,128)(2,1)S(1)}, u32[]{:S(2)}, u32[]{:S(2)}) collective-permute-start(bf16[16,48,1152]{2,1,0:T(8,128)(2,1)S(1)} %get-tuple-element.118), channel_id=1, source_target_pairs={{0,1},{1,0},{2,3},{3,2},{4,5},{5,4},{6,7},{7,6},{8,9},{9,8},{10,11... | collective-permute-start | bytes 5308424 | tf_op jit(solution)/shard_map/ppermute | solution.py:590
  118.3 17.1 %collective-permute-start.13 = (bf16[2,48,1536]{2,1,0:T(8,128)(2,1)S(1)}, bf16[2,48,1536]{2,1,0:T(8,128)(2,1)S(1)}, u32[]{:S(2)}, u32[]{:S(2)}) collective-permute-start(bf16[2,48,1536]{2,1,0:T(8,128)(2,1)S(1)} %get-tuple-element.181), channel_id=1, source_target_pairs={{0,8},{1,9},{2,10},{3,11},{4,12},{5,13},{6,14},{7,15},{8,0},{9,1},... | collective-permute-start | bytes 884744 | tf_op jit(solution)/shard_map/ppermute | solution.py:587
  120.2 19.0 %collective-permute-start.15 = (bf16[4,48,1920]{2,1,0:T(8,128)(2,1)S(1)}, bf16[4,48,1920]{2,1,0:T(8,128)(2,1)S(1)}, u32[]{:S(2)}, u32[]{:S(2)}) collective-permute-start(bf16[4,48,1920]{2,1,0:T(8,128)(2,1)S(1)} %get-tuple-element.173), channel_id=1, source_target_pairs={{0,4},{1,3},{2,6},{3,1},{4,0},{5,7},{6,2},{7,5},{8,12},{9,11},{10,... | collective-permute-start | bytes 2211848 | tf_op jit(solution)/shard_map/ppermute | solution.py:587
  135.5 14.8 %collective-permute-start.18 = (bf16[1024,768]{1,0:T(8,128)(2,1)S(1)}, bf16[1024,768]{1,0:T(8,128)(2,1)S(1)}, u32[]{:S(2)}, u32[]{:S(2)}) collective-permute-start(bf16[1024,768]{1,0:T(8,128)(2,1)S(1)} %get-tuple-element.127), channel_id=1, source_target_pairs={{0,1},{1,0},{2,3},{3,2},{4,5},{5,4},{6,7},{7,6},{8,9},{9,8},{10,11... | collective-permute-start | bytes 4718600 | tf_op jit(solution)/shard_map/ppermute | solution.py:590
  136.1 13.4 %collective-permute-start.17 = (bf16[8,48,1152]{2,1,0:T(8,128)(2,1)S(1)}, bf16[8,48,1152]{2,1,0:T(8,128)(2,1)S(1)}, u32[]{:S(2)}, u32[]{:S(2)}) collective-permute-start(bf16[8,48,1152]{2,1,0:T(8,128)(2,1)S(1)} %get-tuple-element.171), channel_id=1, source_target_pairs={{0,2},{1,5},{2,0},{3,7},{4,6},{5,1},{6,4},{7,3},{8,10},{9,13},{10,... | collective-permute-start | bytes 2654216 | tf_op jit(solution)/shard_map/ppermute | solution.py:587
  136.7 23.4 %collective-permute-start.22 = (bf16[1,48,1536]{2,1,0:T(8,128)(2,1)S(1)}, bf16[1,48,1536]{2,1,0:T(8,128)(2,1)S(1)}, u32[]{:S(2)}, u32[]{:S(2)}) collective-permute-start(bf16[1,48,1536]{2,1,0:T(8,128)(2,1)S(1)} %get-tuple-element.189), channel_id=1, source_target_pairs={{0,16},{1,17},{2,18},{3,19},{4,20},{5,21},{6,22},{7,23},{8,24},{9,... | collective-permute-start | bytes 442376 | tf_op jit(solution)/shard_map/ppermute | solution.py:587
  139.4 14.8 %collective-permute-start.20 = (bf16[2,48,1920]{2,1,0:T(8,128)(2,1)S(1)}, bf16[2,48,1920]{2,1,0:T(8,128)(2,1)S(1)}, u32[]{:S(2)}, u32[]{:S(2)}) collective-permute-start(bf16[2,48,1920]{2,1,0:T(8,128)(2,1)S(1)} %get-tuple-element.179), channel_id=1, source_target_pairs={{0,8},{1,9},{2,10},{3,11},{4,12},{5,13},{6,14},{7,15},{8,0},{9,1},... | collective-permute-start | bytes 1105928 | tf_op jit(solution)/shard_map/ppermute | solution.py:587
  141.0 11.6 %collective-permute-start.19 = (f32[56,128]{1,0:T(8,128)S(1)}, f32[56,128]{1,0:T(8,128)S(1)}, u32[]{:S(2)}, u32[]{:S(2)}) collective-permute-start(f32[56,128]{1,0:T(8,128)S(1)} %add.118), channel_id=1, source_target_pairs={{0,2},{2,0},{4,6},{6,4},{8,10},{10,8},{12,14},{14,12},{16,18},{18,... | collective-permute-start | bytes 86024 | tf_op jit(solution)/shard_map/ppermute | solution.py:663
  149.7 8.7 %collective-permute-start.21 = (bf16[4,48,1152]{2,1,0:T(8,128)(2,1)S(1)}, bf16[4,48,1152]{2,1,0:T(8,128)(2,1)S(1)}, u32[]{:S(2)}, u32[]{:S(2)}) collective-permute-start(bf16[4,48,1152]{2,1,0:T(8,128)(2,1)S(1)} %get-tuple-element.177), channel_id=1, source_target_pairs={{0,4},{1,3},{2,6},{3,1},{4,0},{5,7},{6,2},{7,5},{8,12},{9,11},{10,... | collective-permute-start | bytes 1327112 | tf_op jit(solution)/shard_map/ppermute | solution.py:587
  152.6 8.2 %collective-permute-start.23 = (f32[56,128]{1,0:T(8,128)S(1)}, f32[56,128]{1,0:T(8,128)S(1)}, u32[]{:S(2)}, u32[]{:S(2)}) collective-permute-start(f32[56,128]{1,0:T(8,128)S(1)} %add.122), channel_id=1, source_target_pairs={{0,4},{2,6},{4,0},{6,2},{8,12},{10,14},{12,8},{14,10},{16,20},{18,... | collective-permute-start | bytes 86024 | tf_op jit(solution)/shard_map/ppermute | solution.py:663
  158.5 11.1 %collective-permute-start.24 = (bf16[2,48,1152]{2,1,0:T(8,128)(2,1)S(1)}, bf16[2,48,1152]{2,1,0:T(8,128)(2,1)S(1)}, u32[]{:S(2)}, u32[]{:S(2)}) collective-permute-start(bf16[2,48,1152]{2,1,0:T(8,128)(2,1)S(1)} %get-tuple-element.185), channel_id=1, source_target_pairs={{0,8},{1,9},{2,10},{3,11},{4,12},{5,13},{6,14},{7,15},{8,0},{9,1},... | collective-permute-start | bytes 663560 | tf_op jit(solution)/shard_map/ppermute | solution.py:587
  160.8 7.4 %collective-permute-start.25 = (f32[56,128]{1,0:T(8,128)S(1)}, f32[56,128]{1,0:T(8,128)S(1)}, u32[]{:S(2)}, u32[]{:S(2)}) collective-permute-start(f32[56,128]{1,0:T(8,128)S(1)} %add.128), channel_id=1, source_target_pairs={{0,8},{2,10},{4,12},{6,14},{8,0},{10,2},{12,4},{14,6},{16,24},{18,... | collective-permute-start | bytes 86024 | tf_op jit(solution)/shard_map/ppermute | solution.py:663
  161.4 9.7 %collective-permute-start.26 = (bf16[1,48,1920]{2,1,0:T(8,128)(2,1)S(1)}, bf16[1,48,1920]{2,1,0:T(8,128)(2,1)S(1)}, u32[]{:S(2)}, u32[]{:S(2)}) collective-permute-start(bf16[1,48,1920]{2,1,0:T(8,128)(2,1)S(1)} %get-tuple-element.187), channel_id=1, source_target_pairs={{0,16},{1,17},{2,18},{3,19},{4,20},{5,21},{6,22},{7,23},{8,24},{9,... | collective-permute-start | bytes 552968 | tf_op jit(solution)/shard_map/ppermute | solution.py:587
  171.8 5.6 %collective-permute-start.28 = (bf16[1,48,1152]{2,1,0:T(8,128)(2,1)S(1)}, bf16[1,48,1152]{2,1,0:T(8,128)(2,1)S(1)}, u32[]{:S(2)}, u32[]{:S(2)}) collective-permute-start(bf16[1,48,1152]{2,1,0:T(8,128)(2,1)S(1)} %get-tuple-element.191), channel_id=1, source_target_pairs={{0,16},{1,17},{2,18},{3,19},{4,20},{5,21},{6,22},{7,23},{8,24},{9,... | collective-permute-start | bytes 331784 | tf_op jit(solution)/shard_map/ppermute | solution.py:587
  (25 other events, 210.1 us)
